TPU v7x, 128 devices: a whole 4x4x4 slice. The times are simulated.
128 devices in a mesh: group: 8 (over x, y_hi), view: 2 (over core), patch: 8 (over z, y_lo).
Axes of the slice: x: 4, y: 4 (y_hi: 2, y_lo: 2; y = y_hi * 2 + y_lo), z: 4, core: 2. Of those that a mesh axis runs over, the one named last changes fastest.
Arguments:
- hidden: bfloat16 [32, 1024, 1024], P(('group', 'view'), 'patch'), parts along dimension 0, may hold values from -10.2 to 10.2
- rays: bfloat16 [32, 1024, 1024], P(('group', 'view'), 'patch'), parts along dimension 0, may hold values from -3 to 3
- view_set: int32 [32], P('group'), parts along dimension 0, may hold values from 0 to 1, as said below
- obs_keys: bfloat16 [3, 1024, 1024], P(None, 'patch'), may hold values from -10 to 10
- obs_values: bfloat16 [3, 1024, 1024], P(None, 'patch'), may hold values from -6 to 6
- w_query: bfloat16 [1024, 1024], replicated, may hold values from -0.25 to 0.25
- w_key: bfloat16 [1024, 1024], replicated, may hold values from -0.3125 to 0.3125
- w_value: bfloat16 [1024, 1024], replicated, may hold values from -0.1875 to 0.1875
- w_out: bfloat16 [1024, 1024], replicated, may hold values from -0.5 to 0.5
Outputs:
- attended: bfloat16 [32, 1024, 1024], P(('group', 'view'), 'patch'), parts along dimension 0
There are 8 independent parts, one for each index of `group`. A program takes and returns all parts, laid end to end along the dimension named above; an argument that names none is the same for every part. Nothing has to cross between parts.
Inputs may be any that keep to these rules, and one draw needn't show every extreme that they name: `view_set`: every set has at least one view.
All inputs are finite; a program needn't handle non-finite values.
Results may differ from a plain program's by a relative error of at most 0.0075.
The roundings to bfloat16 on the way count: a program that leaves them out, or rounds other values in their place, can miss the bound.
Values may be sent and summed in bfloat16 or wider, within the bound.
No kernel may reach another device: no remote copies, remote signals or barrier semaphores. Data moves between devices by JAX's collectives and lax.ppermute only.
A program may use at most 320 MiB of HBM per device.

v0:
```python
import math

import jax
import jax.numpy as jnp
from jax import lax
from jax.sharding import PartitionSpec as P

HEADS = 16
HEAD_DIM = 64


def project(rows, weight):
    return jnp.dot(rows, weight, preferred_element_type=jnp.float32).astype(jnp.bfloat16)


def lookup_set(views, view_set):
    table = jnp.arange(view_set.shape[0], dtype=jnp.int32)
    return jnp.sum(jnp.where(views[:, None] == table[None, :], view_set[None, :], 0), axis=1)


def attend(queries, keys, values, query_view, key_view, obs_k, obs_v, view_set):
    count, heads_here, width = queries.shape
    factor = 1.0 / math.sqrt(width)
    block = math.gcd(count, 512)
    key_set = lookup_set(key_view, view_set)
    query_set = lookup_set(query_view, view_set).reshape(count // block, block)
    query_blocks = queries.reshape(count // block, block, heads_here, width)

    def one_block(pair):
        q_block, set_block = pair
        scores = (
            jnp.einsum("qhd,khd->hqk", q_block, keys, preferred_element_type=jnp.float32) * factor
        )
        scores = jnp.where((set_block[:, None] == key_set[None, :])[None], scores, -1e30)
        obs_scores = (
            jnp.einsum("qhd,khd->hqk", q_block, obs_k, preferred_element_type=jnp.float32) * factor
        )
        top = jnp.maximum(jnp.max(scores, axis=2), jnp.max(obs_scores, axis=2))
        weights = jnp.exp(scores - top[:, :, None])
        observed_probabilities = jnp.exp(obs_scores - top[:, :, None])
        total = jnp.sum(weights, axis=2) + jnp.sum(observed_probabilities, axis=2)
        blended_output = jnp.einsum(
            "hqk,khd->qhd", weights.astype(jnp.bfloat16), values, preferred_element_type=jnp.float32
        )
        blended_output = blended_output + jnp.einsum(
            "hqk,khd->qhd",
            observed_probabilities.astype(jnp.bfloat16),
            obs_v,
            preferred_element_type=jnp.float32,
        )
        return (blended_output / total.T[:, :, None]).astype(jnp.bfloat16)

    result = lax.map(one_block, (query_blocks, query_set))
    return result.reshape(count, heads_here, width)


def on_device(hidden, rays, view_set, obs_keys, obs_values, w_query, w_key, w_value, w_out):
    view_dev, tok_dev, width = hidden.shape
    rows = view_dev * tok_dev
    patches = lax.axis_size("patch")
    views_axis = lax.axis_size("view")
    view_here = lax.axis_index("view")
    obs_count = obs_keys.shape[0]
    source = (
        (hidden.astype(jnp.float32) + rays.astype(jnp.float32))
        .astype(jnp.bfloat16)
        .reshape(rows, width)
    )
    queries = project(source, w_query)
    keys = project(source, w_key)
    values = project(source, w_value)
    stacked = jnp.stack((queries, keys, values)).reshape(3, rows, HEADS, HEAD_DIM)
    moved = lax.all_to_all(stacked, ("view", "patch"), split_axis=2, concat_axis=1, tiled=True)
    heads_here = moved.shape[2]
    index = jnp.arange(moved.shape[1], dtype=jnp.int32)
    token_view = index // rows // patches * view_dev + index % rows // tok_dev
    half = width // views_axis
    obs_k = lax.dynamic_slice_in_dim(obs_keys, view_here * half, half, 2)
    obs_v = lax.dynamic_slice_in_dim(obs_values, view_here * half, half, 2)
    obs_k = obs_k.reshape(obs_count, tok_dev, patches, half // patches)
    obs_v = obs_v.reshape(obs_count, tok_dev, patches, half // patches)
    obs_k, obs_v = (
        lax.all_to_all(obs_k, "patch", split_axis=2, concat_axis=1, tiled=True),
        lax.all_to_all(obs_v, "patch", split_axis=2, concat_axis=1, tiled=True),
    )
    obs_k = obs_k.reshape(-1, heads_here, HEAD_DIM)
    obs_v = obs_v.reshape(-1, heads_here, HEAD_DIM)
    context = attend(moved[0], moved[1], moved[2], token_view, token_view, obs_k, obs_v, view_set)
    context = lax.all_to_all(context, ("view", "patch"), split_axis=0, concat_axis=1, tiled=True)
    context = context.reshape(rows, width)
    attended = jnp.dot(context, w_out, preferred_element_type=jnp.float32).astype(jnp.bfloat16)
    return attended.reshape(view_dev, tok_dev, width)


def solution(mesh):
    return jax.shard_map(
        on_device,
        mesh=mesh,
        in_specs=(
            P(("group", "view"), "patch", None),
            P(("group", "view"), "patch", None),
            P("group"),
            P(None, "patch", None),
            P(None, "patch", None),
            P(),
            P(),
            P(),
            P(),
        ),
        out_specs=P(("group", "view"), "patch", None),
        check_vma=False,
    )
```

profile of v0, /device:TPU:27, one launch (start us, length us, event | category | flops | bytes accessed | tf_op | source)
XLA Modules:
  0.0 219.5 jit_solution(8581623216819346196)
XLA Ops:
  0.0 2.1 constant_dynamic-slice_fusion.1
  3.1 6.2 %all-to-all-start.1 = ((bf16[3,128,8,64]{1,3,0,2:T(8,128)(2,1)}), bf16[3,128,8,64]{1,3,0,2:T(8,128)(2,1)S(1)}, u32[]{:S(2)}, u32[]{:S(2)}) async-start(bf16[3,128,8,64]{1,3,0,2:T(8,128)(2,1)} %copy.51), calls=%async_computation.1 | async-start | bytes 786432 | tf_op jit(solution)/shard_map/all_to_all | solution.py:83
  13.5 3.1 %convolution_convert_fusion.2 = bf16[256,1024]{1,0:T(8,128)(2,1)} fusion(bf16[256,1024]{1,0:T(8,128)(2,1)S(1)} %bitcast.129, bf16[1024,1024]{1,0:T(8,128)(2,1)} %param.17), kind=kOutput, calls=%fused_computation.33 | convolution fusion | flops 537133056 | bytes 3145728 | tf_op jit(solution)/shard_map/dot_general | solution.py:13
  17.8 1.9 copy.65
  19.7 1.8 copy.55
  21.5 5.1 %all-to-all-start.2 = ((bf16[3,128,8,64]{1,3,0,2:T(8,128)(2,1)}), bf16[3,128,8,64]{1,3,0,2:T(8,128)(2,1)}, u32[]{:S(2)}, u32[]{:S(2)}) async-start(bf16[3,128,8,64]{1,3,0,2:T(8,128)(2,1)} %copy.55), calls=%async_computation.2 | async-start | bytes 786432 | tf_op jit(solution)/shard_map/all_to_all | solution.py:84
  26.7 3.3 %convolution_convert_fusion.1 = bf16[256,1024]{1,0:T(8,128)(2,1)} fusion(bf16[256,1024]{1,0:T(8,128)(2,1)} %bitcast.130, bf16[1024,1024]{1,0:T(8,128)(2,1)} %param.18), kind=kOutput, calls=%fused_computation.32 | convolution fusion | flops 537133056 | bytes 3145728 | tf_op jit(solution)/shard_map/dot_general | solution.py:13
  29.9 2.0 copy.46
  34.4 7.2 %all-to-all-start = ((bf16[3,256,16,64]{1,3,0,2:T(8,128)(2,1)}), bf16[3,256,16,64]{1,3,0,2:T(8,128)(2,1)}, u32[]{:S(2)}, u32[]{:S(2)}) async-start(bf16[3,256,16,64]{1,3,0,2:T(8,128)(2,1)} %copy.47), calls=%async_computation | async-start | bytes 3145728 | tf_op jit(solution)/shard_map/all_to_all | solution.py:73
  44.9 17.2 %all-to-all-done = bf16[3,256,16,64]{1,3,0,2:T(8,128)(2,1)} async-done(((bf16[3,256,16,64]{1,3,0,2:T(8,128)(2,1)}), bf16[3,256,16,64]{1,3,0,2:T(8,128)(2,1)}, u32[]{:S(2)}, u32[]{:S(2)}) %all-to-all-start) | async-done | bytes 1572896 | tf_op jit(solution)/shard_map/all_to_all | solution.py:73
  62.1 2.5 %fusion.59 = (bf16[1,16,256,1,64]{2,4,0,1,3:T(8,128)(2,1)}, bf16[1,16,256,1,64]{2,4,0,1,3:T(8,128)(2,1)}, bf16[1,16,256,1,64]{2,4,0,1,3:T(8,128)(2,1)S(1)}) fusion(bf16[3,16,256,1,64]{2,4,0,1,3:T(8,128)(2,1)} %bitcast.15), kind=kLoop, calls=%fused_computation.72 | loop fusion | bytes 3145728 | tf_op jit(solution)/shard_map/slice | solution.py:88
  65.9 2.0 copy.57
  70.3 2.1 copy.53
  73.7 89.3 %while.10 = (s32[]{:T(128)}, bf16[8,512,1,64]{1,3,2,0:T(8,128)(2,1)}, s32[8,512]{1,0:T(8,128)}, s32[4096]{0:T(1024)S(1)}, bf16[8,512,1,64]{1,3,2,0:T(8,128)(2,1)...) while((s32[]{:T(128)}, ...), condition=%wide.region_6.7_spmd, body=%wide.region_1.6_spmd.sunk | while | flops 968981504 | bytes 46388840 | solution.py:53
  74.4 2.6 %fusion.81 = (f32[512]{0:T(512)S(1)}, f32[512,4096]{1,0:T(8,128)S(1)}) fusion(bf16[4096,1,64]{0,2,1:T(8,128)(2,1)} %get-tuple-element.195, bf16[8,512,1,64]{1,3,2,0:T(8,128)(2,1)} %get-tuple-element.194, s32[]{:T(128)} %get-tuple-element.180, s32[4096]{0:T(1024)S(1)} %get-tuple-element.193, s32[512]{0:T(512)S(1)} %bitcast.131), kind=kOutput, calls=%fused_computation.71.clone.1 | convolution fusion | flops 276823552 | bytes 8999424 | tf_op jit(solution)/shard_map/while/body/eval_jaxpr/qhd,khd->hqk/dot_general | solution.py:32
  77.0 1.9 multiply_reduce_fusion.2
  81.4 1.5 fusion.82
  83.0 1.9 fusion.85
  85.6 2.6 %fusion.81 = (f32[512]{0:T(512)S(1)}, f32[512,4096]{1,0:T(8,128)S(1)}) fusion(bf16[4096,1,64]{0,2,1:T(8,128)(2,1)} %get-tuple-element.195, bf16[8,512,1,64]{1,3,2,0:T(8,128)(2,1)} %get-tuple-element.194, s32[]{:T(128)} %get-tuple-element.180, s32[4096]{0:T(1024)S(1)} %get-tuple-element.193, s32[512]{0:T(512)S(1)} %bitcast.131), kind=kOutput, calls=%fused_computation.71.clone.1 | convolution fusion | flops 276823552 | bytes 8999424 | tf_op jit(solution)/shard_map/while/body/eval_jaxpr/qhd,khd->hqk/dot_general | solution.py:32
  88.2 1.9 multiply_reduce_fusion.2
  94.1 1.9 fusion.85
  96.8 2.6 %fusion.81 = (f32[512]{0:T(512)S(1)}, f32[512,4096]{1,0:T(8,128)S(1)}) fusion(bf16[4096,1,64]{0,2,1:T(8,128)(2,1)} %get-tuple-element.195, bf16[8,512,1,64]{1,3,2,0:T(8,128)(2,1)} %get-tuple-element.194, s32[]{:T(128)} %get-tuple-element.180, s32[4096]{0:T(1024)S(1)} %get-tuple-element.193, s32[512]{0:T(512)S(1)} %bitcast.131), kind=kOutput, calls=%fused_computation.71.clone.1 | convolution fusion | flops 276823552 | bytes 8999424 | tf_op jit(solution)/shard_map/while/body/eval_jaxpr/qhd,khd->hqk/dot_general | solution.py:32
  99.4 1.9 multiply_reduce_fusion.2
  105.3 1.9 fusion.85
  107.9 2.6 %fusion.81 = (f32[512]{0:T(512)S(1)}, f32[512,4096]{1,0:T(8,128)S(1)}) fusion(bf16[4096,1,64]{0,2,1:T(8,128)(2,1)} %get-tuple-element.195, bf16[8,512,1,64]{1,3,2,0:T(8,128)(2,1)} %get-tuple-element.194, s32[]{:T(128)} %get-tuple-element.180, s32[4096]{0:T(1024)S(1)} %get-tuple-element.193, s32[512]{0:T(512)S(1)} %bitcast.131), kind=kOutput, calls=%fused_computation.71.clone.1 | convolution fusion | flops 276823552 | bytes 8999424 | tf_op jit(solution)/shard_map/while/body/eval_jaxpr/qhd,khd->hqk/dot_general | solution.py:32
  110.5 1.9 multiply_reduce_fusion.2
  114.9 1.5 fusion.82
  116.5 1.9 fusion.85
  119.1 2.6 %fusion.81 = (f32[512]{0:T(512)S(1)}, f32[512,4096]{1,0:T(8,128)S(1)}) fusion(bf16[4096,1,64]{0,2,1:T(8,128)(2,1)} %get-tuple-element.195, bf16[8,512,1,64]{1,3,2,0:T(8,128)(2,1)} %get-tuple-element.194, s32[]{:T(128)} %get-tuple-element.180, s32[4096]{0:T(1024)S(1)} %get-tuple-element.193, s32[512]{0:T(512)S(1)} %bitcast.131), kind=kOutput, calls=%fused_computation.71.clone.1 | convolution fusion | flops 276823552 | bytes 8999424 | tf_op jit(solution)/shard_map/while/body/eval_jaxpr/qhd,khd->hqk/dot_general | solution.py:32
  121.7 1.9 multiply_reduce_fusion.2
  126.1 1.5 fusion.82
  127.6 1.9 fusion.85
  130.3 2.6 %fusion.81 = (f32[512]{0:T(512)S(1)}, f32[512,4096]{1,0:T(8,128)S(1)}) fusion(bf16[4096,1,64]{0,2,1:T(8,128)(2,1)} %get-tuple-element.195, bf16[8,512,1,64]{1,3,2,0:T(8,128)(2,1)} %get-tuple-element.194, s32[]{:T(128)} %get-tuple-element.180, s32[4096]{0:T(1024)S(1)} %get-tuple-element.193, s32[512]{0:T(512)S(1)} %bitcast.131), kind=kOutput, calls=%fused_computation.71.clone.1 | convolution fusion | flops 276823552 | bytes 8999424 | tf_op jit(solution)/shard_map/while/body/eval_jaxpr/qhd,khd->hqk/dot_general | solution.py:32
  132.9 1.9 multiply_reduce_fusion.2
  137.3 1.5 fusion.82
  138.8 1.9 fusion.85
  141.4 2.6 %fusion.81 = (f32[512]{0:T(512)S(1)}, f32[512,4096]{1,0:T(8,128)S(1)}) fusion(bf16[4096,1,64]{0,2,1:T(8,128)(2,1)} %get-tuple-element.195, bf16[8,512,1,64]{1,3,2,0:T(8,128)(2,1)} %get-tuple-element.194, s32[]{:T(128)} %get-tuple-element.180, s32[4096]{0:T(1024)S(1)} %get-tuple-element.193, s32[512]{0:T(512)S(1)} %bitcast.131), kind=kOutput, calls=%fused_computation.71.clone.1 | convolution fusion | flops 276823552 | bytes 8999424 | tf_op jit(solution)/shard_map/while/body/eval_jaxpr/qhd,khd->hqk/dot_general | solution.py:32
  144.0 1.9 multiply_reduce_fusion.2
  150.0 1.9 fusion.85
  152.6 2.6 %fusion.81 = (f32[512]{0:T(512)S(1)}, f32[512,4096]{1,0:T(8,128)S(1)}) fusion(bf16[4096,1,64]{0,2,1:T(8,128)(2,1)} %get-tuple-element.195, bf16[8,512,1,64]{1,3,2,0:T(8,128)(2,1)} %get-tuple-element.194, s32[]{:T(128)} %get-tuple-element.180, s32[4096]{0:T(1024)S(1)} %get-tuple-element.193, s32[512]{0:T(512)S(1)} %bitcast.131), kind=kOutput, calls=%fused_computation.71.clone.1 | convolution fusion | flops 276823552 | bytes 8999424 | tf_op jit(solution)/shard_map/while/body/eval_jaxpr/qhd,khd->hqk/dot_general | solution.py:32
  155.2 1.9 multiply_reduce_fusion.2
  161.1 1.9 fusion.85
  164.6 3.2 %reshape.174 = bf16[4096,1,64]{2,1,0:T(2,128)(2,1)} reshape(bf16[8,512,1,64]{3,1,0,2:T(8,128)(2,1)S(1)} %copy.62) | data formatting | bytes 1048576 | tf_op jit(solution)/shard_map/reshape | solution.py:54
  168.2 23.7 %reduce.8 = bf16[4096,64]{1,0:T(8,128)(2,1)S(1)} reduce(bf16[4096,1,64]{2,1,0:T(2,128)(2,1)} %reshape.174, bf16[]{:T(256)} %broadcast.148), dimensions={1}, to_apply=%reshape.174.reduce_sub_computation | reduce | bytes 1048578 | tf_op jit(solution)/shard_map/reshape | solution.py:54
  193.4 14.5 %all_to_all.60 = bf16[16,2,8192]{2,1,0:T(2,128)(2,1)S(1)} all-to-all(bf16[16,2,8192]{2,1,0:T(2,128)(2,1)} %reshape.175), channel_id=1, replica_groups=mesh['group'=8,'view'=2,'patch'=8] {'view','patch'}, dimensions={0} | all-to-all | bytes 1048576 | tf_op jit(solution)/shard_map/all_to_all | solution.py:89
  208.0 3.6 %reshape.176 = bf16[4096,1,64]{2,1,0:T(2,128)(2,1)} reshape(bf16[16,2,8192]{2,1,0:T(2,128)(2,1)S(1)} %all_to_all.60) | data formatting | bytes 1048576
  211.5 4.6 %copy.60 = bf16[4096,1,64]{0,2,1:T(8,128)(2,1)S(1)} copy(bf16[4096,1,64]{2,1,0:T(2,128)(2,1)} %reshape.176) | data formatting | bytes 1048576 | tf_op jit(solution)/shard_map/all_to_all | solution.py:89
  216.4 3.1 %convolution_convert_fusion = bf16[256,1024]{1,0:T(8,128)(2,1)} fusion(bf16[256,1024]{0,1:T(8,128)(2,1)S(1)} %bitcast.124, bf16[1024,1024]{1,0:T(8,128)(2,1)} %param.19), kind=kOutput, calls=%fused_computation.31 | convolution fusion | flops 537133056 | bytes 3145728 | tf_op jit(solution)/shard_map/dot_general | solution.py:91
  (76 shorter events, 52.4 us)
Async XLA Ops:
  0.0 10.7 %copy-start = (bf16[1024,1024]{1,0:T(8,128)(2,1)S(1)}, bf16[1024,1024]{1,0:T(8,128)(2,1)}, u32[]{:S(2)}) copy-start(bf16[1024,1024]{1,0:T(8,128)(2,1)} %param.16) | copy-start | bytes 6291460
  3.1 18.4 %all-to-all-start.1 = ((bf16[3,128,8,64]{1,3,0,2:T(8,128)(2,1)}), bf16[3,128,8,64]{1,3,0,2:T(8,128)(2,1)S(1)}, u32[]{:S(2)}, u32[]{:S(2)}) async-start(bf16[3,128,8,64]{1,3,0,2:T(8,128)(2,1)} %copy.51), calls=%async_computation.1 | async-start | bytes 786432 | tf_op jit(solution)/shard_map/all_to_all | solution.py:83
  10.7 2.8 %copy-start.1 = (bf16[2,128,1024]{2,1,0:T(8,128)(2,1)}, bf16[2,128,1024]{2,1,0:T(8,128)(2,1)S(1)}, u32[]{:S(2)}) copy-start(bf16[2,128,1024]{2,1,0:T(8,128)(2,1)S(1)} %add_convert_fusion) | copy-start | bytes 1572868
  21.5 12.9 %all-to-all-start.2 = ((bf16[3,128,8,64]{1,3,0,2:T(8,128)(2,1)}), bf16[3,128,8,64]{1,3,0,2:T(8,128)(2,1)}, u32[]{:S(2)}, u32[]{:S(2)}) async-start(bf16[3,128,8,64]{1,3,0,2:T(8,128)(2,1)} %copy.55), calls=%async_computation.2 | async-start | bytes 786432 | tf_op jit(solution)/shard_map/all_to_all | solution.py:84
  34.4 27.7 %all-to-all-start = ((bf16[3,256,16,64]{1,3,0,2:T(8,128)(2,1)}), bf16[3,256,16,64]{1,3,0,2:T(8,128)(2,1)}, u32[]{:S(2)}, u32[]{:S(2)}) async-start(bf16[3,256,16,64]{1,3,0,2:T(8,128)(2,1)} %copy.47), calls=%async_computation | async-start | bytes 3145728 | tf_op jit(solution)/shard_map/all_to_all | solution.py:73
where the time goes:
time: 223 us; the launch traced here: 220 us
  matrix products  74.8 us (34%)
  local copies, waits for them, and re-layouts  47.5 us (21%)
  other arithmetic  46.7 us (21%)
  starting transfers between devices  18.5 us (8%)
  waiting for transfers between devices  17.2 us (8%)
  blocking collectives  14.5 us (7%)
    reshape x1, other arithmetic, attend(): return result.reshape(count, heads_here, width)  23.7 us
    dot_general x8, matrix products, one_block(): jnp.einsum('qhd,khd->hqk', q_block, keys, preferred_element_type=jnp.floa...  20.9 us
    reduce_sum x16, other arithmetic, one_block(): total = jnp.sum(weights, axis=2) + jnp.sum(observed_probabilities, axis=2)  19.6 us
    all_to_all x1, waiting for transfers between devices, on_device(): lax.all_to_all(stacked, ('view', 'patch'), split_axis=2, concat_axis=1, t...  17.2 us
    dot_general x8, matrix products, one_block(): jnp.einsum('qhd,khd->hqk', q_block, obs_k, preferred_element_type=jnp.flo...  15.4 us
    dot_general x8, matrix products, one_block(): jnp.einsum('hqk,khd->qhd', observed_probabilities.astype(jnp.bfloat16), o...  15.3 us
    all_to_all x1, blocking collectives, on_device(): lax.all_to_all(context, ('view', 'patch'), split_axis=0, concat_axis=1, t...  14.5 us
    dot_general x8, matrix products, one_block(): jnp.einsum('hqk,khd->qhd', weights.astype(jnp.bfloat16), values, preferre...  12.2 us
  transfers between devices with their start and end apart: 3, of which 1 were waited for; matrix products, arithmetic and copies ran while one was open for 11% of the time, Pallas kernels for 0%

commit v1 on v0

v1 whole, which is shorter than its diff:
```python
import functools

import jax
import jax.numpy as jnp
from jax import lax
from jax.experimental import pallas as pl
from jax.experimental.pallas import tpu as pltpu
from jax.sharding import PartitionSpec as P

HEADS = 16
HEAD_DIM = 64
SUM_ROW = HEAD_DIM
VALUE_ROWS = HEAD_DIM + 16
KEY_COLS = 2 * HEAD_DIM
LIMIT = 2.0**100
BF16 = jnp.bfloat16
F32 = jnp.float32
MIB = 2**20


def dot(a, b):
    return jnp.dot(a, b, preferred_element_type=F32)


def params(mib):
    return pltpu.CompilerParams(vmem_limit_bytes=mib * MIB)


def cost(flops, nbytes):
    return pl.CostEstimate(flops=int(flops), bytes_accessed=int(nbytes), transcendentals=0)


def make_source(hidden, rays, source):
    both = hidden[...].astype(F32) + rays[...].astype(F32)
    source[...] = both.astype(BF16).reshape(source.shape)


def project_heads(source, weight, scale):
    rows = dot(source[...], weight[...]).astype(BF16)
    if scale != 1.0:
        rows = rows * jnp.asarray(scale, BF16)
    return rows.T


def pack_queries_kernel(view, hidden, rays, weight, obs_k, obs_v, out, source):
    step = pl.program_id(0)

    @pl.when(step == 0)
    def _():
        make_source(hidden, rays, source)

    tok = hidden.shape[1]
    feats = project_heads(source, weight, HEAD_DIM**-0.5)
    for head in range(out.shape[0]):
        rows = slice(head * HEAD_DIM, (head + 1) * HEAD_DIM)
        for i in range(hidden.shape[0]):
            out[head, i * HEAD_DIM : (i + 1) * HEAD_DIM, :] = feats[rows, i * tok : (i + 1) * tok]
    base = hidden.shape[0] * HEAD_DIM

    def observed(ref):
        for o in range(ref.shape[0]):
            turned = ref[o].T
            for head in range(out.shape[0]):
                out[head, base + o * HEAD_DIM : base + (o + 1) * HEAD_DIM, :] = turned[
                    head * HEAD_DIM : (head + 1) * HEAD_DIM
                ]

    @pl.when(view[0] == 0)
    def _():
        observed(obs_k)

    @pl.when(view[0] != 0)
    def _():
        observed(obs_v)


def pack_queries(view, hidden, rays, weight, obs_k, obs_v):
    views, tok, width = hidden.shape
    obs = obs_k.shape[0]
    steps = 4
    cols = width // steps
    heads = HEADS // steps
    rows = (views + obs) * HEAD_DIM
    whole = pl.BlockSpec((views, tok, width), lambda j, v: (0, 0, 0))
    return pl.pallas_call(
        pack_queries_kernel,
        grid_spec=pltpu.PrefetchScalarGridSpec(
            num_scalar_prefetch=1,
            grid=(steps,),
            in_specs=[
                whole,
                whole,
                pl.BlockSpec((width, cols), lambda j, v: (0, j)),
                pl.BlockSpec((obs, tok, cols), lambda j, v: (0, 0, j * (1 - v[0]))),
                pl.BlockSpec((obs, tok, cols), lambda j, v: (0, 0, j * v[0])),
            ],
            out_specs=pl.BlockSpec((heads, rows, tok), lambda j, v: (j, 0, 0)),
            scratch_shapes=[pltpu.VMEM((views * tok, width), BF16)],
        ),
        out_shape=jax.ShapeDtypeStruct((HEADS, rows, tok), BF16),
        compiler_params=params(24),
        cost_estimate=cost(2 * views * tok * width * width, 6 * MIB),
        name="pack_queries",
    )(view, hidden, rays, weight, obs_k, obs_v)


def pack_pairs_kernel(hidden, rays, w_key, w_value, out, source):
    @pl.when(pl.program_id(0) == 0)
    def _():
        make_source(hidden, rays, source)

    views, tok = hidden.shape[:2]
    for place, weight in enumerate((w_key, w_value)):
        feats = project_heads(source, weight, 1.0)
        for head in range(out.shape[0]):
            rows = slice(head * HEAD_DIM, (head + 1) * HEAD_DIM)
            for i in range(views):
                at = (place * views + i) * HEAD_DIM
                out[head, at : at + HEAD_DIM, :] = feats[rows, i * tok : (i + 1) * tok]


def pack_pairs(hidden, rays, w_key, w_value):
    views, tok, width = hidden.shape
    steps = 4
    cols = width // steps
    heads = HEADS // steps
    rows = 2 * views * HEAD_DIM
    whole = pl.BlockSpec((views, tok, width), lambda j: (0, 0, 0))
    column = pl.BlockSpec((width, cols), lambda j: (0, j))
    return pl.pallas_call(
        pack_pairs_kernel,
        grid=(steps,),
        in_specs=[whole, whole, column, column],
        out_specs=pl.BlockSpec((heads, rows, tok), lambda j: (j, 0, 0)),
        scratch_shapes=[pltpu.VMEM((views * tok, width), BF16)],
        out_shape=jax.ShapeDtypeStruct((HEADS, rows, tok), BF16),
        compiler_params=params(24),
        cost_estimate=cost(4 * views * tok * width * width, 7 * MIB),
        name="pack_pairs",
    )(hidden, rays, w_key, w_value)


def ones_rows(count, ones, lanes):
    row = lax.broadcasted_iota(jnp.int32, (count, lanes), 0)
    return jnp.where(row < ones, 1.0, 0.0).astype(BF16)


def store_keys(keys, at, turned):
    tok = turned.shape[1]
    full = jnp.concatenate([turned, ones_rows(KEY_COLS - HEAD_DIM, 3, tok)], axis=0)
    keys[at : at + tok, :] = full.T


def offset_rows(top):
    first = top.astype(BF16)
    rest = top - first.astype(F32)
    second = rest.astype(BF16)
    third = rest - second.astype(F32)
    row = lax.broadcasted_iota(jnp.int32, (KEY_COLS - HEAD_DIM, top.shape[1]), 0)
    picked = jnp.where(row == 0, first.astype(F32), 0.0)
    picked = jnp.where(row == 1, second.astype(F32), picked)
    picked = jnp.where(row == 2, third, picked)
    return (-picked).astype(BF16)


def block_max(keys, at, count, block, query, top):
    def step(i, top):
        start = pl.multiple_of(at + i * block, block)
        scores = dot(keys[pl.ds(start, block), :], query)
        return jnp.maximum(top, jnp.max(scores, axis=0, keepdims=True))

    return lax.fori_loop(0, count // block, step, top)


def weighted(keys, values, start, count, query):
    weights = jnp.exp(dot(keys[pl.ds(start, count), :], query)).astype(BF16)
    return dot(values[:, pl.ds(start, count)], weights)


def observed_kernel(packed, query_out, sums, keys, values):
    patches = packed.shape[0] // 2
    tok = packed.shape[2]
    views = query_out.shape[0]
    here = views // 2
    obs = packed.shape[1] // HEAD_DIM - here
    span = patches * tok
    for o in range(obs):
        rows = slice((here + o) * HEAD_DIM, (here + o + 1) * HEAD_DIM)
        for p in range(patches):
            at = (o * patches + p) * tok
            store_keys(keys, at, packed[p, rows, :])
            values[0:HEAD_DIM, at : at + tok] = packed[patches + p, rows, :]
    values[HEAD_DIM:, :] = jnp.ones((VALUE_ROWS - HEAD_DIM, obs * span), BF16)
    for u in range(views):
        rows = slice((u % here) * HEAD_DIM, (u % here + 1) * HEAD_DIM)
        query = jnp.concatenate([packed[(u // here) * patches + p, rows, :] for p in range(patches)], axis=1)
        query_out[u, 0:HEAD_DIM, :] = query
        top = jnp.max(dot(keys[0:tok, 0:HEAD_DIM], query), axis=0, keepdims=True)
        query_out[u, HEAD_DIM:, :] = offset_rows(top)

    def one_view(u, block):
        query = query_out[u]
        total = None
        for o in range(obs * span // block):
            term = weighted(keys, values, o * block, block, query)
            total = term if total is None else total + term
        sums[u] = total

    @pl.loop(0, views)
    def _(u):
        one_view(u, span)

    largest = jnp.max(sums[:, SUM_ROW : SUM_ROW + 1, :])

    @pl.when(jnp.logical_not(largest < LIMIT))
    def _():
        @pl.loop(0, views)
        def _(u):
            query_out[u, HEAD_DIM:, :] = jnp.zeros((KEY_COLS - HEAD_DIM, span), BF16)
            low = jnp.full((1, span), -jnp.inf, F32)
            top = block_max(keys, 0, obs * span, tok, query_out[u], low)
            query_out[u, HEAD_DIM:, :] = offset_rows(top)
            sums[u] = jnp.zeros(sums.shape[1:], F32)

            @pl.loop(0, obs * patches)
            def _(i):
                sums[u] += weighted(keys, values, pl.multiple_of(i * tok, tok), tok, query_out[u])


def observed_part(packed, views, obs):
    sources, rows, tok = packed.shape
    span = sources // 2 * tok
    return pl.pallas_call(
        observed_kernel,
        out_shape=[
            jax.ShapeDtypeStruct((views, KEY_COLS, span), BF16),
            jax.ShapeDtypeStruct((views, VALUE_ROWS, span), F32),
        ],
        scratch_shapes=[
            pltpu.VMEM((obs * span, KEY_COLS), BF16),
            pltpu.VMEM((VALUE_ROWS, obs * span), BF16),
        ],
        compiler_params=params(40),
        cost_estimate=cost(8 * views * obs * span * span * HEAD_DIM, 4 * MIB),
        name="observed_part",
    )(packed)


def generated_kernel(view_set, query, before, packed, out, keys, values, sums, pairs):
    patches = packed.shape[0] // 2
    tok = packed.shape[2]
    views = query.shape[0]
    here = views // 2
    span = patches * tok
    count = jnp.int32(0)
    for u in range(views):
        for w in range(views):
            pairs[count] = u * views + w
            count = count + (view_set[u] == view_set[w]).astype(jnp.int32)
    for w in range(views):
        k_rows = slice((w % here) * HEAD_DIM, (w % here + 1) * HEAD_DIM)
        v_rows = slice((here + w % here) * HEAD_DIM, (here + w % here + 1) * HEAD_DIM)
        for p in range(patches):
            at = (w * patches + p) * tok
            store_keys(keys, at, packed[(w // here) * patches + p, k_rows, :])
            values[0:HEAD_DIM, at : at + tok] = packed[(w // here) * patches + p, v_rows, :]
    values[HEAD_DIM:, :] = jnp.ones((VALUE_ROWS - HEAD_DIM, views * span), BF16)
    sums[...] = before[...]

    def one_pair(i):
        u = pairs[i] // views
        start = pl.multiple_of((pairs[i] % views) * span, span)
        return u, weighted(keys, values, start, span, query[u])

    @pl.loop(0, count // 2)
    def _(i):
        u0, term0 = one_pair(2 * i)
        u1, term1 = one_pair(2 * i + 1)
        sums[u0] += term0
        sums[u1] += term1

    largest = jnp.max(sums[:, SUM_ROW : SUM_ROW + 1, :])

    @pl.when(jnp.logical_not(largest < LIMIT))
    def _():
        @pl.loop(0, views)
        def _(u):
            rows = -query[u, HEAD_DIM : HEAD_DIM + 16, :].astype(F32)
            old = rows[0:1] + rows[1:2] + rows[2:3]
            plain = jnp.concatenate(
                [query[u, 0:HEAD_DIM, :], jnp.zeros((KEY_COLS - HEAD_DIM, span), BF16)], axis=0
            )

            def look(w, top):
                seen = jnp.where(view_set[u] == view_set[w], span, 0)
                return block_max(keys, w * span, seen, tok, plain, top)

            top = lax.fori_loop(0, views, look, old)
            shifted = jnp.concatenate([query[u, 0:HEAD_DIM, :], offset_rows(top)], axis=0)
            sums[u] = before[u] * jnp.exp(old - top)

            @pl.loop(0, views)
            def _(w):
                @pl.when(view_set[u] == view_set[w])
                def _():
                    @pl.loop(0, patches)
                    def _(p):
                        start = pl.multiple_of(w * span + p * tok, tok)
                        sums[u] += weighted(keys, values, start, tok, shifted)

    for u in range(views):
        total = sums[u]
        context = (total[0:HEAD_DIM] / total[SUM_ROW : SUM_ROW + 1]).astype(BF16)
        rows = slice((u % here) * HEAD_DIM, (u % here + 1) * HEAD_DIM)
        for p in range(patches):
            out[(u // here) * patches + p, rows, :] = context[:, p * tok : (p + 1) * tok]


def generated_part(view_set, query, before, packed):
    sources, rows, tok = packed.shape
    views, _, span = query.shape
    vmem = pl.BlockSpec(memory_space=pltpu.VMEM)
    return pl.pallas_call(
        generated_kernel,
        in_specs=[pl.BlockSpec(memory_space=pltpu.SMEM), vmem, vmem, vmem],
        out_shape=jax.ShapeDtypeStruct((sources, rows // 2, tok), BF16),
        scratch_shapes=[
            pltpu.VMEM((views * span, KEY_COLS), BF16),
            pltpu.VMEM((VALUE_ROWS, views * span), BF16),
            pltpu.VMEM((views, VALUE_ROWS, span), F32),
            pltpu.SMEM((views * views + 1,), jnp.int32),
        ],
        compiler_params=params(40),
        cost_estimate=cost(6 * views * views * span * span * HEAD_DIM, 4 * MIB),
        name="generated_part",
    )(view_set, query, before, packed)


def project_out_kernel(packed, weight, out, context):
    views, tok = out.shape[:2]

    @pl.when(pl.program_id(0) == 0)
    def _():
        for i in range(views):
            rows = packed[:, i * HEAD_DIM : (i + 1) * HEAD_DIM, :].reshape(HEADS * HEAD_DIM, tok)
            context[i * tok : (i + 1) * tok, :] = rows.T

    out[...] = dot(context[...], weight[...]).astype(BF16).reshape(out.shape)


def project_out(packed, weight):
    heads, rows, tok = packed.shape
    views = rows // HEAD_DIM
    width = weight.shape[0]
    steps = 2
    cols = width // steps
    return pl.pallas_call(
        project_out_kernel,
        grid=(steps,),
        in_specs=[
            pl.BlockSpec((heads, rows, tok), lambda j: (0, 0, 0)),
            pl.BlockSpec((width, cols), lambda j: (0, j)),
        ],
        out_specs=pl.BlockSpec((views, tok, cols), lambda j: (0, 0, j)),
        out_shape=jax.ShapeDtypeStruct((views, tok, width), BF16),
        scratch_shapes=[pltpu.VMEM((views * tok, width), BF16)],
        compiler_params=params(24),
        cost_estimate=cost(2 * views * tok * width * width, 4 * MIB),
        name="project_out",
    )(packed, weight)


def exchange(blocks):
    return lax.all_to_all(blocks, ("view", "patch"), split_axis=0, concat_axis=0, tiled=True)


def on_device(hidden, rays, view_set, obs_keys, obs_values, w_query, w_key, w_value, w_out):
    views = view_set.shape[0]
    view = lax.axis_index("view").astype(jnp.int32).reshape(1)
    queries = exchange(pack_queries(view, hidden, rays, w_query, obs_keys, obs_values))
    pairs = exchange(pack_pairs(hidden, rays, w_key, w_value))
    query, before = observed_part(queries, views, obs_keys.shape[0])
    context = exchange(generated_part(view_set, query, before, pairs))
    return project_out(context, w_out)


def solution(mesh):
    return jax.shard_map(
        on_device,
        mesh=mesh,
        in_specs=(
            P(("group", "view"), "patch", None),
            P(("group", "view"), "patch", None),
            P("group"),
            P(None, "patch", None),
            P(None, "patch", None),
            P(),
            P(),
            P(),
            P(),
        ),
        out_specs=P(("group", "view"), "patch", None),
        check_vma=False,
    )
```

time: 223 us -> 184 us (0.83)
  the two profiles are of different devices: /device:TPU:27 before, /device:TPU:2 now
where the time goes in v1:
time: 184 us
  Pallas kernels  136 us (74%)
  blocking collectives  15.7 us (9%)
  waiting for transfers between devices  13 us (7%)
  starting transfers between devices  10.9 us (6%)
  local copies, waits for them, and re-layouts  7.55 us (4%)
    pallas_call x1, Pallas kernels, observed_part(): pl.pallas_call(observed_kernel, out_shape=[jax.ShapeDtypeStruct((views, K...  70.6 us
    pallas_call x1, Pallas kernels, generated_part(): pl.pallas_call(generated_kernel, in_specs=[pl.BlockSpec(memory_space=pltp...  57.1 us
    all_to_all x1, blocking collectives, exchange(): lax.all_to_all(blocks, ('view', 'patch'), split_axis=0, concat_axis=0, ti...  15.7 us
    all_to_all x2, waiting for transfers between devices, exchange(): lax.all_to_all(blocks, ('view', 'patch'), split_axis=0, concat_axis=0, ti...  13 us
    all_to_all x2, starting transfers between devices, exchange(): lax.all_to_all(blocks, ('view', 'patch'), split_axis=0, concat_axis=0, ti...  10.9 us
    unnamed x22, local copies, waits for them, and re-layouts  7.55 us
  transfers between devices with their start and end apart: 2, of which 1 were waited for; matrix products, arithmetic and copies ran while one was open for 0% of the time, Pallas kernels for 40%

profile of v1, /device:TPU:2, one launch (start us, length us, event | category | flops | bytes accessed | tf_op | source)
XLA Modules:
  0.0 183.7 jit_solution(13479364946803882563)
XLA Ops:
  0.0 0.0 copy-start
  0.0 1.6 copy-done
  1.6 0.0 copy-start.3
  1.6 1.0 copy-done.3
  2.6 0.0 copy-start.5
  2.6 1.0 copy-done.5
  3.7 0.0 copy-start.8
  3.7 1.1 copy-done.8
  4.8 0.0 copy-start.9
  4.8 1.1 copy-done.9
  5.9 0.0 copy-start.6
  5.9 3.3 %pack_queries.1 = bf16[16,320,128]{2,1,0:T(8,128)(2,1)} custom-call(s32[1]{0:T(128)} %bitcast.view, bf16[2,128,1024]{2,1,0:T(8,128)(2,1)S(1)} %copy-done.3, bf16[2,128,1024]{2,1,0:T(8,128)(2,1)S(1)} %copy-done.5, bf16[1024,1024]{1,0:T(8,128)(2,1)S(1)} %copy-done, bf16[3,128,1024]{2,1,0:T(8,128)(2,1)S(1)} %copy-done.8, bf16[3,128,1024]{2,1,0:T(8,128)(2,1)S(1)} %copy-done.9), custom_call_target="tpu_custom_call" | custom-call | flops 536870912 | bytes 6291456 | tf_op jit(solution)/shard_map/pack_queries/pallas_call | solution.py:85
  9.2 0.0 copy-start.1
  9.2 0.0 copy-start.4
  9.2 6.7 %all-to-all-start = ((bf16[16,320,128]{2,1,0:T(8,128)(2,1)}), bf16[16,320,128]{2,1,0:T(8,128)(2,1)}, u32[]{:S(2)}, u32[]{:S(2)}) async-start(bf16[16,320,128]{2,1,0:T(8,128)(2,1)} %pack_queries.1), calls=%async_computation | async-start | bytes 2621440 | tf_op jit(solution)/shard_map/all_to_all | solution.py:374
  16.0 0.0 copy-done.6
  16.0 0.0 copy-done.1
  16.0 0.0 copy-done.4
  16.0 0.0 copy-start.2
  16.0 1.6 copy-done.2
  17.6 3.5 %pack_pairs.1 = bf16[16,256,128]{2,1,0:T(8,128)(2,1)} custom-call(bf16[2,128,1024]{2,1,0:T(8,128)(2,1)S(1)} %copy-done.4, bf16[2,128,1024]{2,1,0:T(8,128)(2,1)S(1)} %copy-done.6, bf16[1024,1024]{1,0:T(8,128)(2,1)S(1)} %copy-done.1, bf16[1024,1024]{1,0:T(8,128)(2,1)S(1)} %copy-done.2), custom_call_target="tpu_custom_call" | custom-call | flops 1073741824 | bytes 7340032 | tf_op jit(solution)/shard_map/pack_pairs/pallas_call | solution.py:130
  21.1 13.0 %all-to-all-done.packed = bf16[16,320,128]{2,1,0:T(8,128)(2,1)} async-done(((bf16[16,320,128]{2,1,0:T(8,128)(2,1)}), bf16[16,320,128]{2,1,0:T(8,128)(2,1)}, u32[]{:S(2)}, u32[]{:S(2)}) %all-to-all-start) | async-done | bytes 1310752 | tf_op jit(solution)/shard_map/all_to_all | solution.py:374
  34.1 4.1 %all-to-all-start.1 = ((bf16[16,256,128]{2,1,0:T(8,128)(2,1)}), bf16[16,256,128]{2,1,0:T(8,128)(2,1)S(1)}, u32[]{:S(2)}, u32[]{:S(2)}) async-start(bf16[16,256,128]{2,1,0:T(8,128)(2,1)} %pack_pairs.1), calls=%async_computation.1 | async-start | bytes 2097152 | tf_op jit(solution)/shard_map/all_to_all | solution.py:374
  38.2 0.0 copy-start.10
  38.3 70.6 %observed_part.1 = (bf16[4,128,1024]{2,1,0:T(8,128)(2,1)S(1)}, f32[4,80,1024]{2,1,0:T(8,128)S(1)}) custom-call(bf16[16,320,128]{2,1,0:T(8,128)(2,1)} %all-to-all-done.packed), custom_call_target="tpu_custom_call" | custom-call | flops 6442450944 | bytes 4194304 | tf_op jit(solution)/shard_map/observed_part/pallas_call | solution.py:233
  108.8 0.0 all-to-all-done.1.packed
  108.8 0.0 copy-done.10
  108.8 0.0 copy-start.7
  108.8 57.1 %generated_part.1 = bf16[16,128,128]{2,1,0:T(8,128)(2,1)S(1)} custom-call(s32[4]{0:T(128)S(1)} %copy-done.10, bf16[4,128,1024]{2,1,0:T(8,128)(2,1)S(1)} %get-tuple-element.7.query, f32[4,80,1024]{2,1,0:T(8,128)S(1)} %get-tuple-element.8.before, bf16[16,256,128]{2,1,0:T(8,128)(2,1)S(1)} %all-to-all-done.1.packed), custom_call_target="tpu_custom_call" | custom-call | flops 6442450944 | bytes 4194304 | tf_op jit(solution)/shard_map/generated_part/pallas_call | solution.py:323
  166.0 15.7 %all_to_all.15.packed = bf16[16,128,128]{2,1,0:T(8,128)(2,1)S(1)} all-to-all(bf16[16,128,128]{2,1,0:T(8,128)(2,1)S(1)} %generated_part.1), channel_id=1, replica_groups=mesh['group'=8,'view'=2,'patch'=8] {'view','patch'}, dimensions={0} | all-to-all | bytes 1048576 | tf_op jit(solution)/shard_map/all_to_all | solution.py:374
  181.7 0.0 copy-done.7
  181.7 1.9 %project_out.1 = bf16[2,128,1024]{2,1,0:T(8,128)(2,1)} custom-call(bf16[16,128,128]{2,1,0:T(8,128)(2,1)S(1)} %all_to_all.15.packed, bf16[1024,1024]{1,0:T(8,128)(2,1)S(1)} %copy-done.7), custom_call_target="tpu_custom_call" | custom-call | flops 536870912 | bytes 4194304 | tf_op jit(solution)/shard_map/project_out/pallas_call | solution.py:357
Async XLA Ops:
  0.0 1.6 copy-start
  1.6 1.0 copy-start.3
  2.6 1.0 copy-start.5
  3.7 1.1 copy-start.8
  4.8 1.1 copy-start.9
  5.9 10.1 %copy-start.6 = (bf16[2,128,1024]{2,1,0:T(8,128)(2,1)S(1)}, bf16[2,128,1024]{2,1,0:T(8,128)(2,1)}, u32[]{:S(2)}) copy-start(bf16[2,128,1024]{2,1,0:T(8,128)(2,1)} %rays.3) | copy-start | bytes 1572868
  9.2 6.8 %copy-start.1 = (bf16[1024,1024]{1,0:T(8,128)(2,1)S(1)}, bf16[1024,1024]{1,0:T(8,128)(2,1)}, u32[]{:S(2)}) copy-start(bf16[1024,1024]{1,0:T(8,128)(2,1)} %w_key.1) | copy-start | bytes 6291460
  9.2 6.8 %copy-start.4 = (bf16[2,128,1024]{2,1,0:T(8,128)(2,1)S(1)}, bf16[2,128,1024]{2,1,0:T(8,128)(2,1)}, u32[]{:S(2)}) copy-start(bf16[2,128,1024]{2,1,0:T(8,128)(2,1)} %hidden.3) | copy-start | bytes 1572868
  9.2 24.9 %all-to-all-start = ((bf16[16,320,128]{2,1,0:T(8,128)(2,1)}), bf16[16,320,128]{2,1,0:T(8,128)(2,1)}, u32[]{:S(2)}, u32[]{:S(2)}) async-start(bf16[16,320,128]{2,1,0:T(8,128)(2,1)} %pack_queries.1), calls=%async_computation | async-start | bytes 2621440 | tf_op jit(solution)/shard_map/all_to_all | solution.py:374
  16.0 1.6 copy-start.2
  34.1 74.7 %all-to-all-start.1 = ((bf16[16,256,128]{2,1,0:T(8,128)(2,1)}), bf16[16,256,128]{2,1,0:T(8,128)(2,1)S(1)}, u32[]{:S(2)}, u32[]{:S(2)}) async-start(bf16[16,256,128]{2,1,0:T(8,128)(2,1)} %pack_pairs.1), calls=%async_computation.1 | async-start | bytes 2097152 | tf_op jit(solution)/shard_map/all_to_all | solution.py:374
  38.2 70.6 %copy-start.10 = (s32[4]{0:T(128)S(1)}, s32[4]{0:T(128)}, u32[]{:S(2)}) copy-start(s32[4]{0:T(128)} %view_set.1) | copy-start | bytes 52
  108.8 72.9 %copy-start.7 = (bf16[1024,1024]{1,0:T(8,128)(2,1)S(1)}, bf16[1024,1024]{1,0:T(8,128)(2,1)}, u32[]{:S(2)}) copy-start(bf16[1024,1024]{1,0:T(8,128)(2,1)} %weight.3) | copy-start | bytes 6291460

commit v2 on v1

v2 whole, which is shorter than its diff:
```python
import jax
import jax.numpy as jnp
from jax import lax
from jax.experimental import pallas as pl
from jax.experimental.pallas import tpu as pltpu
from jax.sharding import PartitionSpec as P

HEADS = 16
HEAD_DIM = 64
SUM_ROW = HEAD_DIM
VALUE_ROWS = HEAD_DIM + 16
KEY_COLS = 2 * HEAD_DIM
LIMIT = 2.0**100
BF16 = jnp.bfloat16
F32 = jnp.float32
MIB = 2**20


def dot(a, b):
    return jnp.dot(a, b, preferred_element_type=F32)


def params(mib):
    return pltpu.CompilerParams(vmem_limit_bytes=mib * MIB)


def cost(flops, nbytes):
    return pl.CostEstimate(flops=int(flops), bytes_accessed=int(nbytes), transcendentals=0)


def pack_kernel(
    view, hidden, rays, w_query, w_key, w_value, obs_k, obs_v, queries, pairs,
    hid, ray, weights, obs, source, query_blocks, pair_blocks, in_sem, out_sem,
):
    views, tok = hidden.shape[:2]
    copies = [pltpu.make_async_copy(hidden, hid, in_sem.at[0]), pltpu.make_async_copy(rays, ray, in_sem.at[1])]
    loads = [
        pltpu.make_async_copy(w, weights.at[i], in_sem.at[2 + i]) for i, w in enumerate((w_query, w_key, w_value))
    ]
    observed = [pltpu.make_async_copy(o, obs, in_sem.at[5]) for o in (obs_k, obs_v)]
    for c in copies:
        c.start()
    loads[0].start()
    for kind in range(2):

        @pl.when(view[0] == kind)
        def _():
            observed[kind].start()

    for c in loads[1:]:
        c.start()
    for c in copies:
        c.wait()
    both = hid[...].astype(F32) + ray[...].astype(F32)
    source[...] = both.astype(BF16).reshape(source.shape)

    def place(blocks, base, feats, count):
        for head in range(HEADS):
            rows = slice(head * HEAD_DIM, (head + 1) * HEAD_DIM)
            for i in range(count):
                at = (base + i) * HEAD_DIM
                blocks[head, at : at + HEAD_DIM, :] = feats[rows, i * tok : (i + 1) * tok]

    def feats_of(i):
        loads[i].wait()
        return dot(source[...], weights[i]).astype(BF16)

    place(query_blocks, 0, (feats_of(0) * jnp.asarray(HEAD_DIM**-0.5, BF16)).T, views)
    observed[0].wait()
    place(query_blocks, views, obs[...].reshape(-1, obs.shape[-1]).T, obs.shape[0])
    sends = [pltpu.make_async_copy(query_blocks, queries, out_sem.at[0])]
    sends[0].start()
    place(pair_blocks, 0, feats_of(1).T, views)
    place(pair_blocks, views, feats_of(2).T, views)
    sends.append(pltpu.make_async_copy(pair_blocks, pairs, out_sem.at[1]))
    sends[1].start()
    for c in sends:
        c.wait()


def pack(view, hidden, rays, w_query, w_key, w_value, obs_k, obs_v):
    views, tok, width = hidden.shape
    query_shape = (HEADS, (views + obs_k.shape[0]) * HEAD_DIM, tok)
    pair_shape = (HEADS, 2 * views * HEAD_DIM, tok)
    hbm = pl.BlockSpec(memory_space=pltpu.MemorySpace.HBM)
    return pl.pallas_call(
        pack_kernel,
        in_specs=[pl.BlockSpec(memory_space=pltpu.SMEM)] + [hbm] * 7,
        out_specs=[hbm, hbm],
        out_shape=[jax.ShapeDtypeStruct(query_shape, BF16), jax.ShapeDtypeStruct(pair_shape, BF16)],
        scratch_shapes=[
            pltpu.VMEM(hidden.shape, BF16),
            pltpu.VMEM(rays.shape, BF16),
            pltpu.VMEM((3,) + w_query.shape, BF16),
            pltpu.VMEM(obs_k.shape, BF16),
            pltpu.VMEM((views * tok, width), BF16),
            pltpu.VMEM(query_shape, BF16),
            pltpu.VMEM(pair_shape, BF16),
            pltpu.SemaphoreType.DMA((6,)),
            pltpu.SemaphoreType.DMA((2,)),
        ],
        compiler_params=params(56),
        cost_estimate=cost(6 * views * tok * width * width, 10 * MIB),
        name="pack",
    )(view, hidden, rays, w_query, w_key, w_value, obs_k, obs_v)


def ones_rows(count, ones, lanes):
    row = lax.broadcasted_iota(jnp.int32, (count, lanes), 0)
    return jnp.where(row < ones, 1.0, 0.0).astype(BF16)


def store_keys(keys, at, turned):
    tok = turned.shape[1]
    full = jnp.concatenate([turned, ones_rows(KEY_COLS - HEAD_DIM, 3, tok)], axis=0)
    keys[at : at + tok, :] = full.T


def offset_rows(top):
    first = top.astype(BF16)
    rest = top - first.astype(F32)
    second = rest.astype(BF16)
    third = rest - second.astype(F32)
    row = lax.broadcasted_iota(jnp.int32, (KEY_COLS - HEAD_DIM, top.shape[1]), 0)
    picked = jnp.where(row == 0, first.astype(F32), 0.0)
    picked = jnp.where(row == 1, second.astype(F32), picked)
    picked = jnp.where(row == 2, third, picked)
    return (-picked).astype(BF16)


def block_max(keys, at, count, block, query, top):
    def step(i, top):
        start = pl.multiple_of(at + i * block, block)
        scores = dot(keys[pl.ds(start, block), :], query)
        return jnp.maximum(top, jnp.max(scores, axis=0, keepdims=True))

    return lax.fori_loop(0, count // block, step, top)


def weighted(keys, values, start, count, query):
    weights = jnp.exp(dot(keys[pl.ds(start, count), :], query)).astype(BF16)
    return dot(values[:, pl.ds(start, count)], weights)


def observed_kernel(packed, query_out, sums_out, keys, values, sums, sems):
    patches = packed.shape[0] // 2
    tok = packed.shape[2]
    views = query_out.shape[0]
    here = views // 2
    obs = packed.shape[1] // HEAD_DIM - here
    span = patches * tok
    for o in range(obs):
        rows = slice((here + o) * HEAD_DIM, (here + o + 1) * HEAD_DIM)
        for p in range(patches):
            at = (o * patches + p) * tok
            store_keys(keys, at, packed[p, rows, :])
            values[0:HEAD_DIM, at : at + tok] = packed[patches + p, rows, :]
    values[HEAD_DIM:, :] = jnp.ones((VALUE_ROWS - HEAD_DIM, obs * span), BF16)
    for u in range(views):
        rows = slice((u % here) * HEAD_DIM, (u % here + 1) * HEAD_DIM)
        query = jnp.concatenate([packed[(u // here) * patches + p, rows, :] for p in range(patches)], axis=1)
        query_out[u, 0:HEAD_DIM, :] = query
        top = jnp.max(dot(keys[0:tok, 0:HEAD_DIM], query), axis=0, keepdims=True)
        query_out[u, HEAD_DIM:, :] = offset_rows(top)

    def one_view(u, block):
        query = query_out[u]
        total = None
        for o in range(obs * span // block):
            term = weighted(keys, values, o * block, block, query)
            total = term if total is None else total + term
        sums[u] = total

    def send(u):
        return pltpu.make_async_copy(sums.at[u], sums_out.at[u], sems.at[u])

    @pl.loop(0, views)
    def _(u):
        one_view(u, span)
        send(u).start()

    largest = jnp.max(sums[:, SUM_ROW : SUM_ROW + 1, :])
    for u in range(views):
        send(u).wait()

    @pl.when(jnp.logical_not(largest < LIMIT))
    def _():
        @pl.loop(0, views)
        def _(u):
            query_out[u, HEAD_DIM:, :] = jnp.zeros((KEY_COLS - HEAD_DIM, span), BF16)
            low = jnp.full((1, span), -jnp.inf, F32)
            top = block_max(keys, 0, obs * span, tok, query_out[u], low)
            query_out[u, HEAD_DIM:, :] = offset_rows(top)
            sums[u] = jnp.zeros(sums.shape[1:], F32)

            @pl.loop(0, obs * patches)
            def _(i):
                sums[u] += weighted(keys, values, pl.multiple_of(i * tok, tok), tok, query_out[u])

            send(u).start()
            send(u).wait()


def observed_part(packed, views, obs):
    sources, rows, tok = packed.shape
    span = sources // 2 * tok
    vmem = pl.BlockSpec(memory_space=pltpu.VMEM)
    return pl.pallas_call(
        observed_kernel,
        in_specs=[vmem],
        out_specs=[vmem, pl.BlockSpec(memory_space=pltpu.MemorySpace.HBM)],
        out_shape=[
            jax.ShapeDtypeStruct((views, KEY_COLS, span), BF16),
            pltpu.MemorySpace.HBM((views, VALUE_ROWS, span), F32),
        ],
        scratch_shapes=[
            pltpu.VMEM((obs * span, KEY_COLS), BF16),
            pltpu.VMEM((VALUE_ROWS, obs * span), BF16),
            pltpu.VMEM((views, VALUE_ROWS, span), F32),
            pltpu.SemaphoreType.DMA((views,)),
        ],
        compiler_params=params(32),
        cost_estimate=cost(8 * views * obs * span * span * HEAD_DIM, 4 * MIB),
        name="observed_part",
    )(packed)


def generated_kernel(view_set, query, before, packed, out, keys, values, sums, pairs, sem):
    patches = packed.shape[0] // 2
    tok = packed.shape[2]
    views = query.shape[0]
    here = views // 2
    span = patches * tok
    fetch = pltpu.make_async_copy(before, sums, sem)
    fetch.start()
    count = jnp.int32(0)
    for u in range(views):
        for w in range(views):
            pairs[count] = u * views + w
            count = count + (view_set[u] == view_set[w]).astype(jnp.int32)
    for w in range(views):
        k_rows = slice((w % here) * HEAD_DIM, (w % here + 1) * HEAD_DIM)
        v_rows = slice((here + w % here) * HEAD_DIM, (here + w % here + 1) * HEAD_DIM)
        for p in range(patches):
            at = (w * patches + p) * tok
            store_keys(keys, at, packed[(w // here) * patches + p, k_rows, :])
            values[0:HEAD_DIM, at : at + tok] = packed[(w // here) * patches + p, v_rows, :]
    values[HEAD_DIM:, :] = jnp.ones((VALUE_ROWS - HEAD_DIM, views * span), BF16)
    fetch.wait()

    def one_pair(i):
        u = pairs[i] // views
        start = pl.multiple_of((pairs[i] % views) * span, span)
        return u, weighted(keys, values, start, span, query[u])

    @pl.loop(0, count // 2)
    def _(i):
        u0, term0 = one_pair(2 * i)
        u1, term1 = one_pair(2 * i + 1)
        sums[u0] += term0
        sums[u1] += term1

    largest = jnp.max(sums[:, SUM_ROW : SUM_ROW + 1, :])

    @pl.when(jnp.logical_not(largest < LIMIT))
    def _():
        again = pltpu.make_async_copy(before, sums, sem)
        again.start()
        again.wait()

        @pl.loop(0, views)
        def _(u):
            rows = -query[u, HEAD_DIM : HEAD_DIM + 16, :].astype(F32)
            old = rows[0:1] + rows[1:2] + rows[2:3]
            plain = jnp.concatenate(
                [query[u, 0:HEAD_DIM, :], jnp.zeros((KEY_COLS - HEAD_DIM, span), BF16)], axis=0
            )

            def look(w, top):
                seen = jnp.where(view_set[u] == view_set[w], span, 0)
                return block_max(keys, w * span, seen, tok, plain, top)

            top = lax.fori_loop(0, views, look, old)
            shifted = jnp.concatenate([query[u, 0:HEAD_DIM, :], offset_rows(top)], axis=0)
            sums[u] = sums[u] * jnp.exp(old - top)

            @pl.loop(0, views)
            def _(w):
                @pl.when(view_set[u] == view_set[w])
                def _():
                    @pl.loop(0, patches)
                    def _(p):
                        start = pl.multiple_of(w * span + p * tok, tok)
                        sums[u] += weighted(keys, values, start, tok, shifted)

    for u in range(views):
        total = sums[u]
        context = (total[0:HEAD_DIM] / total[SUM_ROW : SUM_ROW + 1]).astype(BF16)
        rows = slice((u % here) * HEAD_DIM, (u % here + 1) * HEAD_DIM)
        for p in range(patches):
            out[(u // here) * patches + p, rows, :] = context[:, p * tok : (p + 1) * tok]


def generated_part(view_set, query, before, packed):
    sources, rows, tok = packed.shape
    views, _, span = query.shape
    vmem = pl.BlockSpec(memory_space=pltpu.VMEM)
    return pl.pallas_call(
        generated_kernel,
        in_specs=[
            pl.BlockSpec(memory_space=pltpu.SMEM),
            vmem,
            pl.BlockSpec(memory_space=pltpu.MemorySpace.HBM),
            vmem,
        ],
        out_specs=vmem,
        out_shape=jax.ShapeDtypeStruct((sources, rows // 2, tok), BF16),
        scratch_shapes=[
            pltpu.VMEM((views * span, KEY_COLS), BF16),
            pltpu.VMEM((VALUE_ROWS, views * span), BF16),
            pltpu.VMEM((views, VALUE_ROWS, span), F32),
            pltpu.SMEM((views * views + 1,), jnp.int32),
            pltpu.SemaphoreType.DMA,
        ],
        compiler_params=params(32),
        cost_estimate=cost(6 * views * views * span * span * HEAD_DIM, 4 * MIB),
        name="generated_part",
    )(view_set, query, pltpu.with_memory_space_constraint(before, pltpu.MemorySpace.HBM), packed)


def project_out_kernel(packed, weight, out, context, blocks, sems):
    views, tok = out.shape[:2]
    for i in range(views):
        rows = packed[:, i * HEAD_DIM : (i + 1) * HEAD_DIM, :].reshape(HEADS * HEAD_DIM, tok)
        context[i * tok : (i + 1) * tok, :] = rows.T
    copies = []
    cols = weight.shape[1] // 2
    for j in range(2):
        at = slice(j * cols, (j + 1) * cols)
        blocks[:, :, at] = dot(context[...], weight[:, at]).astype(BF16).reshape(views, tok, cols)
        copies.append(pltpu.make_async_copy(blocks.at[:, :, at], out.at[:, :, at], sems.at[j]))
        copies[j].start()
    for c in copies:
        c.wait()


def project_out(packed, weight):
    heads, rows, tok = packed.shape
    views = rows // HEAD_DIM
    width = weight.shape[0]
    vmem = pl.BlockSpec(memory_space=pltpu.VMEM)
    return pl.pallas_call(
        project_out_kernel,
        in_specs=[vmem, vmem],
        out_specs=pl.BlockSpec(memory_space=pltpu.MemorySpace.HBM),
        out_shape=jax.ShapeDtypeStruct((views, tok, width), BF16),
        scratch_shapes=[
            pltpu.VMEM((views * tok, width), BF16),
            pltpu.VMEM((views, tok, width), BF16),
            pltpu.SemaphoreType.DMA((2,)),
        ],
        compiler_params=params(24),
        cost_estimate=cost(2 * views * tok * width * width, 4 * MIB),
        name="project_out",
    )(packed, weight)


def exchange(blocks):
    return lax.all_to_all(blocks, ("view", "patch"), split_axis=0, concat_axis=0, tiled=True)


def on_device(hidden, rays, view_set, obs_keys, obs_values, w_query, w_key, w_value, w_out):
    views = view_set.shape[0]
    view = lax.axis_index("view").astype(jnp.int32).reshape(1)
    queries, pairs = pack(view, hidden, rays, w_query, w_key, w_value, obs_keys, obs_values)
    queries = exchange(queries)
    pairs = exchange(pairs)
    query, before = observed_part(queries, views, obs_keys.shape[0])
    context = exchange(generated_part(view_set, query, before, pairs))
    return project_out(context, w_out)


def solution(mesh):
    return jax.shard_map(
        on_device,
        mesh=mesh,
        in_specs=(
            P(("group", "view"), "patch", None),
            P(("group", "view"), "patch", None),
            P("group"),
            P(None, "patch", None),
            P(None, "patch", None),
            P(),
            P(),
            P(),
            P(),
        ),
        out_specs=P(("group", "view"), "patch", None),
        check_vma=False,
    )
```

time: 184 us -> 185 us (level)
  the two profiles are of different devices: /device:TPU:2 before, /device:TPU:27 now
where the time goes in v2:
time: 185 us; the launch traced here: 184 us
  blocking collectives  97.5 us (53%)
  Pallas kernels  79 us (43%)
  starting transfers between devices  5.39 us (3%)
  waiting for transfers between devices  2.12 us (1%)
    all_to_all x2, blocking collectives, exchange(): lax.all_to_all(blocks, ('view', 'patch'), split_axis=0, concat_axis=0, ti...  97.5 us
    pallas_call x1, Pallas kernels, generated_part(): pl.pallas_call(generated_kernel, in_specs=[pl.BlockSpec(memory_space=pltp...  59.3 us
    pallas_call x1, Pallas kernels, observed_part(): pl.pallas_call(observed_kernel, in_specs=[vmem], out_specs=[vmem, pl.Bloc...  12.7 us
    pallas_call x1, Pallas kernels, pack(): pl.pallas_call(pack_kernel, in_specs=[pl.BlockSpec(memory_space=pltpu.SME...  5.58 us
    all_to_all x1, starting transfers between devices, exchange(): lax.all_to_all(blocks, ('view', 'patch'), split_axis=0, concat_axis=0, ti...  5.39 us
  transfers between devices with their start and end apart: 1, of which 1 were waited for; matrix products, arithmetic and copies ran while one was open for 0% of the time, Pallas kernels for 7%

profile of v2, /device:TPU:27, one launch (start us, length us, event | category | flops | bytes accessed | tf_op | source)
XLA Modules:
  0.0 184.1 jit_solution(17133972545981323295)
XLA Ops:
  0.0 5.6 %pack.1 = (bf16[16,320,128]{2,1,0:T(8,128)(2,1)}, bf16[16,256,128]{2,1,0:T(8,128)(2,1)}) custom-call(s32[1]{0:T(128)} %bitcast.view, bf16[2,128,1024]{2,1,0:T(8,128)(2,1)} %hidden.1, bf16[2,128,1024]{2,1,0:T(8,128)(2,1)} %rays.1, bf16[1024,1024]{1,0:T(8,128)(2,1)} %w_query.1, bf16[1024,1024]{1,0:T(8,128)(2,1)} %w_key.1, bf16[1024,1024]{1,0:T(8,128)(2,1)} %w_value.1, ...), custom_call_target="tpu_custom_call" | custom-call | flops 1610612736 | bytes 10485760 | tf_op jit(solution)/shard_map/pack/pallas_call | solution.py:86
  5.6 24.5 %all_to_all.15.packed = bf16[16,320,128]{2,1,0:T(8,128)(2,1)S(1)} all-to-all(bf16[16,320,128]{2,1,0:T(8,128)(2,1)} %get-tuple-element.9), channel_id=1, replica_groups=mesh['group'=8,'view'=2,'patch'=8] {'view','patch'}, dimensions={0} | all-to-all | bytes 2621440 | tf_op jit(solution)/shard_map/all_to_all | solution.py:369
  30.1 5.4 %all-to-all-start.1 = ((bf16[16,256,128]{2,1,0:T(8,128)(2,1)}), bf16[16,256,128]{2,1,0:T(8,128)(2,1)S(1)}, u32[]{:S(2)}, u32[]{:S(2)}) async-start(bf16[16,256,128]{2,1,0:T(8,128)(2,1)} %get-tuple-element.12), calls=%async_computation.1 | async-start | bytes 2097152 | tf_op jit(solution)/shard_map/all_to_all | solution.py:369
  35.5 0.0 copy-start.1
  35.5 12.7 %observed_part.1 = (bf16[4,128,1024]{2,1,0:T(8,128)(2,1)S(1)}, f32[4,80,1024]{2,1,0:T(8,128)}) custom-call(bf16[16,320,128]{2,1,0:T(8,128)(2,1)S(1)} %all_to_all.15.packed), custom_call_target="tpu_custom_call" | custom-call | flops 6442450944 | bytes 4194304 | tf_op jit(solution)/shard_map/observed_part/pallas_call | solution.py:208
  48.2 2.1 %all-to-all-done.1.packed = bf16[16,256,128]{2,1,0:T(8,128)(2,1)S(1)} async-done(((bf16[16,256,128]{2,1,0:T(8,128)(2,1)}), bf16[16,256,128]{2,1,0:T(8,128)(2,1)S(1)}, u32[]{:S(2)}, u32[]{:S(2)}) %all-to-all-start.1) | async-done | bytes 1048608 | tf_op jit(solution)/shard_map/all_to_all | solution.py:369
  50.3 0.0 copy-done.1
  50.3 0.0 copy-start
  50.3 59.3 %generated_part.1 = bf16[16,128,128]{2,1,0:T(8,128)(2,1)S(1)} custom-call(s32[4]{0:T(128)S(1)} %copy-done.1, bf16[4,128,1024]{2,1,0:T(8,128)(2,1)S(1)} %get-tuple-element.10.query, f32[4,80,1024]{2,1,0:T(8,128)} %get-tuple-element.11.before, bf16[16,256,128]{2,1,0:T(8,128)(2,1)S(1)} %all-to-all-done.1.packed), custom_call_target="tpu_custom_call" | custom-call | flops 6442450944 | bytes 4194304 | tf_op jit(solution)/shard_map/generated_part/pallas_call | solution.py:308
  109.6 73.0 %all_to_all.16.packed = bf16[16,128,128]{2,1,0:T(8,128)(2,1)S(1)} all-to-all(bf16[16,128,128]{2,1,0:T(8,128)(2,1)S(1)} %generated_part.1), channel_id=1, replica_groups=mesh['group'=8,'view'=2,'patch'=8] {'view','patch'}, dimensions={0} | all-to-all | bytes 1048576 | tf_op jit(solution)/shard_map/all_to_all | solution.py:369
  182.6 0.0 copy-done
  182.6 1.5 project_out.1
Async XLA Ops:
  30.1 20.2 %all-to-all-start.1 = ((bf16[16,256,128]{2,1,0:T(8,128)(2,1)}), bf16[16,256,128]{2,1,0:T(8,128)(2,1)S(1)}, u32[]{:S(2)}, u32[]{:S(2)}) async-start(bf16[16,256,128]{2,1,0:T(8,128)(2,1)} %get-tuple-element.12), calls=%async_computation.1 | async-start | bytes 2097152 | tf_op jit(solution)/shard_map/all_to_all | solution.py:369
  35.5 14.8 %copy-start.1 = (s32[4]{0:T(128)S(1)}, s32[4]{0:T(128)}, u32[]{:S(2)}) copy-start(s32[4]{0:T(128)} %view_set.1) | copy-start | bytes 52
  50.3 132.3 %copy-start = (bf16[1024,1024]{1,0:T(8,128)(2,1)S(1)}, bf16[1024,1024]{1,0:T(8,128)(2,1)}, u32[]{:S(2)}) copy-start(bf16[1024,1024]{1,0:T(8,128)(2,1)} %weight.1) | copy-start | bytes 6291460

commit v3 on v2

--- a/solution.py
+++ b/solution.py
@@ -28,81 +28,139 @@
     return pl.CostEstimate(flops=int(flops), bytes_accessed=int(nbytes), transcendentals=0)
 
 
-def pack_kernel(
-    view, hidden, rays, w_query, w_key, w_value, obs_k, obs_v, queries, pairs,
-    hid, ray, weights, obs, source, query_blocks, pair_blocks, in_sem, out_sem,
+HBM = pl.BlockSpec(memory_space=pltpu.MemorySpace.HBM)
+COLUMNS = 2
+
+
+def column_loads(weight, held, sems, first):
+    cols = weight.shape[1] // COLUMNS
+    return [
+        pltpu.make_async_copy(
+            weight.at[:, j * cols : (j + 1) * cols], held.at[:, j * cols : (j + 1) * cols], sems.at[first + j]
+        )
+        for j in range(COLUMNS)
+    ]
+
+
+def make_source(hid, ray, source):
+    both = hid[...].astype(F32) + ray[...].astype(F32)
+    source[...] = both.astype(BF16).reshape(source.shape)
+
+
+def place(blocks, first, base, feats, count, tok):
+    for head in range(feats.shape[0] // HEAD_DIM):
+        rows = slice(head * HEAD_DIM, (head + 1) * HEAD_DIM)
+        for i in range(count):
+            at = (base + i) * HEAD_DIM
+            blocks[first + head, at : at + HEAD_DIM, :] = feats[rows, i * tok : (i + 1) * tok]
+
+
+def pack_queries_kernel(
+    view, hidden, rays, weight, obs_k, obs_v, out, hid, ray, held, obs, source, blocks, in_sem, out_sem
 ):
     views, tok = hidden.shape[:2]
-    copies = [pltpu.make_async_copy(hidden, hid, in_sem.at[0]), pltpu.make_async_copy(rays, ray, in_sem.at[1])]
-    loads = [
-        pltpu.make_async_copy(w, weights.at[i], in_sem.at[2 + i]) for i, w in enumerate((w_query, w_key, w_value))
-    ]
-    observed = [pltpu.make_async_copy(o, obs, in_sem.at[5]) for o in (obs_k, obs_v)]
-    for c in copies:
-        c.start()
-    loads[0].start()
+    inputs = [pltpu.make_async_copy(hidden, hid, in_sem.at[0]), pltpu.make_async_copy(rays, ray, in_sem.at[1])]
+    observed = [pltpu.make_async_copy(o, obs, in_sem.at[2]) for o in (obs_k, obs_v)]
+    columns = column_loads(weight, held, in_sem, 3)
     for kind in range(2):
 
         @pl.when(view[0] == kind)
         def _():
             observed[kind].start()
 
-    for c in loads[1:]:
+    for c in inputs + columns:
         c.start()
-    for c in copies:
+    base = views * HEAD_DIM
+    sends = []
+
+    def send(place_of):
+        sends.append(pltpu.make_async_copy(blocks.at[place_of], out.at[place_of], out_sem.at[len(sends)]))
+        sends[-1].start()
+
+    observed[0].wait()
+    place(blocks, 0, views, obs[...].reshape(-1, obs.shape[-1]).T, obs.shape[0], tok)
+    send((slice(None), slice(base, None)))
+    for c in inputs:
         c.wait()
-    both = hid[...].astype(F32) + ray[...].astype(F32)
-    source[...] = both.astype(BF16).reshape(source.shape)
-
-    def place(blocks, base, feats, count):
-        for head in range(HEADS):
-            rows = slice(head * HEAD_DIM, (head + 1) * HEAD_DIM)
-            for i in range(count):
-                at = (base + i) * HEAD_DIM
-                blocks[head, at : at + HEAD_DIM, :] = feats[rows, i * tok : (i + 1) * tok]
-
-    def feats_of(i):
-        loads[i].wait()
-        return dot(source[...], weights[i]).astype(BF16)
-
-    place(query_blocks, 0, (feats_of(0) * jnp.asarray(HEAD_DIM**-0.5, BF16)).T, views)
-    observed[0].wait()
-    place(query_blocks, views, obs[...].reshape(-1, obs.shape[-1]).T, obs.shape[0])
-    sends = [pltpu.make_async_copy(query_blocks, queries, out_sem.at[0])]
-    sends[0].start()
-    place(pair_blocks, 0, feats_of(1).T, views)
-    place(pair_blocks, views, feats_of(2).T, views)
-    sends.append(pltpu.make_async_copy(pair_blocks, pairs, out_sem.at[1]))
-    sends[1].start()
+    make_source(hid, ray, source)
+    cols = weight.shape[1] // COLUMNS
+    heads = HEADS // COLUMNS
+    for j in range(COLUMNS):
+        columns[j].wait()
+        feats = dot(source[...], held[:, j * cols : (j + 1) * cols]).astype(BF16) * jnp.asarray(HEAD_DIM**-0.5, BF16)
+        place(blocks, j * heads, 0, feats.T, views, tok)
+        send((slice(j * heads, (j + 1) * heads), slice(0, base)))
     for c in sends:
         c.wait()
 
 
-def pack(view, hidden, rays, w_query, w_key, w_value, obs_k, obs_v):
+def pack_queries(view, hidden, rays, weight, obs_k, obs_v):
     views, tok, width = hidden.shape
-    query_shape = (HEADS, (views + obs_k.shape[0]) * HEAD_DIM, tok)
-    pair_shape = (HEADS, 2 * views * HEAD_DIM, tok)
-    hbm = pl.BlockSpec(memory_space=pltpu.MemorySpace.HBM)
+    shape = (HEADS, (views + obs_k.shape[0]) * HEAD_DIM, tok)
     return pl.pallas_call(
-        pack_kernel,
-        in_specs=[pl.BlockSpec(memory_space=pltpu.SMEM)] + [hbm] * 7,
-        out_specs=[hbm, hbm],
-        out_shape=[jax.ShapeDtypeStruct(query_shape, BF16), jax.ShapeDtypeStruct(pair_shape, BF16)],
+        pack_queries_kernel,
+        in_specs=[pl.BlockSpec(memory_space=pltpu.SMEM)] + [HBM] * 5,
+        out_specs=HBM,
+        out_shape=jax.ShapeDtypeStruct(shape, BF16),
         scratch_shapes=[
             pltpu.VMEM(hidden.shape, BF16),
             pltpu.VMEM(rays.shape, BF16),
-            pltpu.VMEM((3,) + w_query.shape, BF16),
+            pltpu.VMEM(weight.shape, BF16),
             pltpu.VMEM(obs_k.shape, BF16),
             pltpu.VMEM((views * tok, width), BF16),
-            pltpu.VMEM(query_shape, BF16),
-            pltpu.VMEM(pair_shape, BF16),
-            pltpu.SemaphoreType.DMA((6,)),
-            pltpu.SemaphoreType.DMA((2,)),
-        ],
-        compiler_params=params(56),
-        cost_estimate=cost(6 * views * tok * width * width, 10 * MIB),
-        name="pack",
-    )(view, hidden, rays, w_query, w_key, w_value, obs_k, obs_v)
+            pltpu.VMEM(shape, BF16),
+            pltpu.SemaphoreType.DMA((3 + COLUMNS,)),
+            pltpu.SemaphoreType.DMA((1 + COLUMNS,)),
+        ],
+        compiler_params=params(58),
+        cost_estimate=cost(2 * views * tok * width * width, 6 * MIB),
+        name="pack_queries",
+    )(view, hidden, rays, weight, obs_k, obs_v)
+
+
+def pack_pairs_kernel(hidden, rays, w_key, w_value, out, hid, ray, held_k, held_v, source, blocks, in_sem, out_sem):
+    views, tok = hidden.shape[:2]
+    inputs = [pltpu.make_async_copy(hidden, hid, in_sem.at[0]), pltpu.make_async_copy(rays, ray, in_sem.at[1])]
+    columns = column_loads(w_key, held_k, in_sem, 2) + column_loads(w_value, held_v, in_sem, 2 + COLUMNS)
+    for c in inputs + columns:
+        c.start()
+    for c in inputs:
+        c.wait()
+    make_source(hid, ray, source)
+    cols = w_key.shape[1] // COLUMNS
+    heads = HEADS // COLUMNS
+    for i, held in enumerate((held_k, held_v)):
+        for j in range(COLUMNS):
+            columns[i * COLUMNS + j].wait()
+            feats = dot(source[...], held[:, j * cols : (j + 1) * cols]).astype(BF16)
+            place(blocks, j * heads, i * views, feats.T, views, tok)
+    send = pltpu.make_async_copy(blocks, out, out_sem)
+    send.start()
+    send.wait()
+
+
+def pack_pairs(hidden, rays, w_key, w_value):
+    views, tok, width = hidden.shape
+    shape = (HEADS, 2 * views * HEAD_DIM, tok)
+    return pl.pallas_call(
+        pack_pairs_kernel,
+        in_specs=[HBM] * 4,
+        out_specs=HBM,
+        out_shape=jax.ShapeDtypeStruct(shape, BF16),
+        scratch_shapes=[
+            pltpu.VMEM(hidden.shape, BF16),
+            pltpu.VMEM(rays.shape, BF16),
+            pltpu.VMEM(w_key.shape, BF16),
+            pltpu.VMEM(w_value.shape, BF16),
+            pltpu.VMEM((views * tok, width), BF16),
+            pltpu.VMEM(shape, BF16),
+            pltpu.SemaphoreType.DMA((2 + 2 * COLUMNS,)),
+            pltpu.SemaphoreType.DMA,
+        ],
+        compiler_params=params(58),
+        cost_estimate=cost(4 * views * tok * width * width, 7 * MIB),
+        name="pack_pairs",
+    )(hidden, rays, w_key, w_value)
 
 
 def ones_rows(count, ones, lanes):
@@ -225,13 +283,13 @@
     )(packed)
 
 
-def generated_kernel(view_set, query, before, packed, out, keys, values, sums, pairs, sem):
+def generated_kernel(view_set, query, before, packed, out, keys, values, sums, pairs, early, sem):
     patches = packed.shape[0] // 2
     tok = packed.shape[2]
     views = query.shape[0]
     here = views // 2
     span = patches * tok
-    fetch = pltpu.make_async_copy(before, sums, sem)
+    fetch = pltpu.make_async_copy(before, early, sem)
     fetch.start()
     count = jnp.int32(0)
     for u in range(views):
@@ -246,7 +304,7 @@
             store_keys(keys, at, packed[(w // here) * patches + p, k_rows, :])
             values[0:HEAD_DIM, at : at + tok] = packed[(w // here) * patches + p, v_rows, :]
     values[HEAD_DIM:, :] = jnp.ones((VALUE_ROWS - HEAD_DIM, views * span), BF16)
-    fetch.wait()
+    sums[...] = jnp.zeros(sums.shape, F32)
 
     def one_pair(i):
         u = pairs[i] // views
@@ -261,13 +319,10 @@
         sums[u1] += term1
 
     largest = jnp.max(sums[:, SUM_ROW : SUM_ROW + 1, :])
+    fetch.wait()
 
     @pl.when(jnp.logical_not(largest < LIMIT))
     def _():
-        again = pltpu.make_async_copy(before, sums, sem)
-        again.start()
-        again.wait()
-
         @pl.loop(0, views)
         def _(u):
             rows = -query[u, HEAD_DIM : HEAD_DIM + 16, :].astype(F32)
@@ -282,7 +337,8 @@
 
             top = lax.fori_loop(0, views, look, old)
             shifted = jnp.concatenate([query[u, 0:HEAD_DIM, :], offset_rows(top)], axis=0)
-            sums[u] = sums[u] * jnp.exp(old - top)
+            early[u] = early[u] * jnp.exp(old - top)
+            sums[u] = jnp.zeros(sums.shape[1:], F32)
 
             @pl.loop(0, views)
             def _(w):
@@ -294,7 +350,7 @@
                         sums[u] += weighted(keys, values, start, tok, shifted)
 
     for u in range(views):
-        total = sums[u]
+        total = sums[u] + early[u]
         context = (total[0:HEAD_DIM] / total[SUM_ROW : SUM_ROW + 1]).astype(BF16)
         rows = slice((u % here) * HEAD_DIM, (u % here + 1) * HEAD_DIM)
         for p in range(patches):
@@ -320,6 +376,7 @@
             pltpu.VMEM((VALUE_ROWS, views * span), BF16),
             pltpu.VMEM((views, VALUE_ROWS, span), F32),
             pltpu.SMEM((views * views + 1,), jnp.int32),
+            pltpu.VMEM((views, VALUE_ROWS, span), F32),
             pltpu.SemaphoreType.DMA,
         ],
         compiler_params=params(32),
@@ -372,9 +429,8 @@
 def on_device(hidden, rays, view_set, obs_keys, obs_values, w_query, w_key, w_value, w_out):
     views = view_set.shape[0]
     view = lax.axis_index("view").astype(jnp.int32).reshape(1)
-    queries, pairs = pack(view, hidden, rays, w_query, w_key, w_value, obs_keys, obs_values)
-    queries = exchange(queries)
-    pairs = exchange(pairs)
+    queries = exchange(pack_queries(view, hidden, rays, w_query, obs_keys, obs_values))
+    pairs = exchange(pack_pairs(hidden, rays, w_key, w_value))
     query, before = observed_part(queries, views, obs_keys.shape[0])
     context = exchange(generated_part(view_set, query, before, pairs))
     return project_out(context, w_out)

time: 185 us -> 180 us (0.973)
  the two profiles are of different devices: /device:TPU:27 before, /device:TPU:6 now
where the time goes in v3:
time: 180 us
  Pallas kernels  140 us (78%)
  blocking collectives  15.7 us (9%)
  waiting for transfers between devices  13.4 us (7%)
  starting transfers between devices  10.6 us (6%)
    pallas_call x1, Pallas kernels, observed_part(): pl.pallas_call(observed_kernel, in_specs=[vmem], out_specs=[vmem, pl.Bloc...  73.2 us
    pallas_call x1, Pallas kernels, generated_part(): pl.pallas_call(generated_kernel, in_specs=[pl.BlockSpec(memory_space=pltp...  57.1 us
    all_to_all x1, blocking collectives, exchange(): lax.all_to_all(blocks, ('view', 'patch'), split_axis=0, concat_axis=0, ti...  15.7 us
    all_to_all x2, waiting for transfers between devices, exchange(): lax.all_to_all(blocks, ('view', 'patch'), split_axis=0, concat_axis=0, ti...  13.4 us
    all_to_all x2, starting transfers between devices, exchange(): lax.all_to_all(blocks, ('view', 'patch'), split_axis=0, concat_axis=0, ti...  10.6 us
    pallas_call x1, Pallas kernels, pack_pairs(): pl.pallas_call(pack_pairs_kernel, in_specs=[HBM] * 4, out_specs=HBM, out_...  4.63 us
  transfers between devices with their start and end apart: 2, of which 1 were waited for; matrix products, arithmetic and copies ran while one was open for 0% of the time, Pallas kernels for 43%

profile of v3, /device:TPU:6, one launch (start us, length us, event | category | flops | bytes accessed | tf_op | source)
XLA Modules:
  0.0 179.7 jit_solution(6641118592701215697)
XLA Ops:
  0.0 3.6 %pack_queries.1 = bf16[16,320,128]{2,1,0:T(8,128)(2,1)} custom-call(s32[1]{0:T(128)} %bitcast.view, bf16[2,128,1024]{2,1,0:T(8,128)(2,1)} %hidden.3, bf16[2,128,1024]{2,1,0:T(8,128)(2,1)} %rays.3, bf16[1024,1024]{1,0:T(8,128)(2,1)} %weight.2, bf16[3,128,1024]{2,1,0:T(8,128)(2,1)} %obs_k.1, bf16[3,128,1024]{2,1,0:T(8,128)(2,1)} %obs_v.1), custom_call_target="tpu_custom_call" | custom-call | flops 536870912 | bytes 6291456 | tf_op jit(solution)/shard_map/pack_queries/pallas_call | solution.py:100
  3.6 6.4 %all-to-all-start = ((bf16[16,320,128]{2,1,0:T(8,128)(2,1)}), bf16[16,320,128]{2,1,0:T(8,128)(2,1)S(1)}, u32[]{:S(2)}, u32[]{:S(2)}) async-start(bf16[16,320,128]{2,1,0:T(8,128)(2,1)} %pack_queries.1), calls=%async_computation | async-start | bytes 2621440 | tf_op jit(solution)/shard_map/all_to_all | solution.py:426
  10.0 4.6 %pack_pairs.1 = bf16[16,256,128]{2,1,0:T(8,128)(2,1)} custom-call(bf16[2,128,1024]{2,1,0:T(8,128)(2,1)} %hidden.3, bf16[2,128,1024]{2,1,0:T(8,128)(2,1)} %rays.3, bf16[1024,1024]{1,0:T(8,128)(2,1)} %w_key.1, bf16[1024,1024]{1,0:T(8,128)(2,1)} %w_value.1), custom_call_target="tpu_custom_call" | custom-call | flops 1073741824 | bytes 7340032 | tf_op jit(solution)/shard_map/pack_pairs/pallas_call | solution.py:145
  14.7 13.4 %all-to-all-done.packed = bf16[16,320,128]{2,1,0:T(8,128)(2,1)S(1)} async-done(((bf16[16,320,128]{2,1,0:T(8,128)(2,1)}), bf16[16,320,128]{2,1,0:T(8,128)(2,1)S(1)}, u32[]{:S(2)}, u32[]{:S(2)}) %all-to-all-start) | async-done | bytes 1310752 | tf_op jit(solution)/shard_map/all_to_all | solution.py:426
  28.1 4.1 %all-to-all-start.1 = ((bf16[16,256,128]{2,1,0:T(8,128)(2,1)}), bf16[16,256,128]{2,1,0:T(8,128)(2,1)S(1)}, u32[]{:S(2)}, u32[]{:S(2)}) async-start(bf16[16,256,128]{2,1,0:T(8,128)(2,1)} %pack_pairs.1), calls=%async_computation.1 | async-start | bytes 2097152 | tf_op jit(solution)/shard_map/all_to_all | solution.py:426
  32.2 0.0 copy-start.1
  32.2 73.2 %observed_part.1 = (bf16[4,128,1024]{2,1,0:T(8,128)(2,1)S(1)}, f32[4,80,1024]{2,1,0:T(8,128)}) custom-call(bf16[16,320,128]{2,1,0:T(8,128)(2,1)S(1)} %all-to-all-done.packed), custom_call_target="tpu_custom_call" | custom-call | flops 6442450944 | bytes 4194304 | tf_op jit(solution)/shard_map/observed_part/pallas_call | solution.py:266
  105.4 0.0 all-to-all-done.1.packed
  105.4 0.0 copy-done.1
  105.4 0.0 copy-start
  105.4 57.1 %generated_part.1 = bf16[16,128,128]{2,1,0:T(8,128)(2,1)S(1)} custom-call(s32[4]{0:T(128)S(1)} %copy-done.1, bf16[4,128,1024]{2,1,0:T(8,128)(2,1)S(1)} %get-tuple-element.7.query, f32[4,80,1024]{2,1,0:T(8,128)} %get-tuple-element.8.before, bf16[16,256,128]{2,1,0:T(8,128)(2,1)S(1)} %all-to-all-done.1.packed), custom_call_target="tpu_custom_call" | custom-call | flops 6442450944 | bytes 4194304 | tf_op jit(solution)/shard_map/generated_part/pallas_call | solution.py:364
  162.6 15.7 %all_to_all.15.packed = bf16[16,128,128]{2,1,0:T(8,128)(2,1)S(1)} all-to-all(bf16[16,128,128]{2,1,0:T(8,128)(2,1)S(1)} %generated_part.1), channel_id=1, replica_groups=mesh['group'=8,'view'=2,'patch'=8] {'view','patch'}, dimensions={0} | all-to-all | bytes 1048576 | tf_op jit(solution)/shard_map/all_to_all | solution.py:426
  178.3 0.0 copy-done
  178.3 1.5 project_out.1
Async XLA Ops:
  3.6 24.5 %all-to-all-start = ((bf16[16,320,128]{2,1,0:T(8,128)(2,1)}), bf16[16,320,128]{2,1,0:T(8,128)(2,1)S(1)}, u32[]{:S(2)}, u32[]{:S(2)}) async-start(bf16[16,320,128]{2,1,0:T(8,128)(2,1)} %pack_queries.1), calls=%async_computation | async-start | bytes 2621440 | tf_op jit(solution)/shard_map/all_to_all | solution.py:426
  28.1 77.3 %all-to-all-start.1 = ((bf16[16,256,128]{2,1,0:T(8,128)(2,1)}), bf16[16,256,128]{2,1,0:T(8,128)(2,1)S(1)}, u32[]{:S(2)}, u32[]{:S(2)}) async-start(bf16[16,256,128]{2,1,0:T(8,128)(2,1)} %pack_pairs.1), calls=%async_computation.1 | async-start | bytes 2097152 | tf_op jit(solution)/shard_map/all_to_all | solution.py:426
  32.2 73.2 %copy-start.1 = (s32[4]{0:T(128)S(1)}, s32[4]{0:T(128)}, u32[]{:S(2)}) copy-start(s32[4]{0:T(128)} %view_set.1) | copy-start | bytes 52
  105.4 72.9 %copy-start = (bf16[1024,1024]{1,0:T(8,128)(2,1)S(1)}, bf16[1024,1024]{1,0:T(8,128)(2,1)}, u32[]{:S(2)}) copy-start(bf16[1024,1024]{1,0:T(8,128)(2,1)} %weight.3) | copy-start | bytes 6291460

commit v4 on v3

--- a/solution.py
+++ b/solution.py
@@ -118,7 +118,9 @@
     )(view, hidden, rays, weight, obs_k, obs_v)
 
 
-def pack_pairs_kernel(hidden, rays, w_key, w_value, out, hid, ray, held_k, held_v, source, blocks, in_sem, out_sem):
+def pack_pairs_kernel(
+    view, hidden, rays, w_key, w_value, keep, give, hid, ray, held_k, held_v, source, blocks, in_sem, out_sem
+):
     views, tok = hidden.shape[:2]
     inputs = [pltpu.make_async_copy(hidden, hid, in_sem.at[0]), pltpu.make_async_copy(rays, ray, in_sem.at[1])]
     columns = column_loads(w_key, held_k, in_sem, 2) + column_loads(w_value, held_v, in_sem, 2 + COLUMNS)
@@ -134,19 +136,25 @@
             columns[i * COLUMNS + j].wait()
             feats = dot(source[...], held[:, j * cols : (j + 1) * cols]).astype(BF16)
             place(blocks, j * heads, i * views, feats.T, views, tok)
-    send = pltpu.make_async_copy(blocks, out, out_sem)
-    send.start()
-    send.wait()
-
-
-def pack_pairs(hidden, rays, w_key, w_value):
+    half = keep.shape[0]
+    sends = [
+        pltpu.make_async_copy(blocks.at[pl.ds(side * half, half)], out, out_sem.at[i])
+        for i, (side, out) in enumerate(((view[0], keep), (1 - view[0], give)))
+    ]
+    for c in sends:
+        c.start()
+    for c in sends:
+        c.wait()
+
+
+def pack_pairs(view, hidden, rays, w_key, w_value):
     views, tok, width = hidden.shape
     shape = (HEADS, 2 * views * HEAD_DIM, tok)
     return pl.pallas_call(
         pack_pairs_kernel,
-        in_specs=[HBM] * 4,
-        out_specs=HBM,
-        out_shape=jax.ShapeDtypeStruct(shape, BF16),
+        in_specs=[pl.BlockSpec(memory_space=pltpu.SMEM)] + [HBM] * 4,
+        out_specs=[HBM, HBM],
+        out_shape=[jax.ShapeDtypeStruct((HEADS // 2,) + shape[1:], BF16)] * 2,
         scratch_shapes=[
             pltpu.VMEM(hidden.shape, BF16),
             pltpu.VMEM(rays.shape, BF16),
@@ -155,12 +163,12 @@
             pltpu.VMEM((views * tok, width), BF16),
             pltpu.VMEM(shape, BF16),
             pltpu.SemaphoreType.DMA((2 + 2 * COLUMNS,)),
-            pltpu.SemaphoreType.DMA,
+            pltpu.SemaphoreType.DMA((2,)),
         ],
         compiler_params=params(58),
         cost_estimate=cost(4 * views * tok * width * width, 7 * MIB),
         name="pack_pairs",
-    )(hidden, rays, w_key, w_value)
+    )(view, hidden, rays, w_key, w_value)
 
 
 def ones_rows(count, ones, lanes):
@@ -283,26 +291,30 @@
     )(packed)
 
 
-def generated_kernel(view_set, query, before, packed, out, keys, values, sums, pairs, early, sem):
-    patches = packed.shape[0] // 2
+def generated_kernel(view_set, view, query, before, packed, out, keys, values, sums, pairs, early, sem):
+    patches = packed.shape[0]
     tok = packed.shape[2]
     views = query.shape[0]
     here = views // 2
     span = patches * tok
     fetch = pltpu.make_async_copy(before, early, sem)
     fetch.start()
+
+    def key_set(w):
+        return view_set[jnp.bitwise_xor(w, here * view[0])]
+
     count = jnp.int32(0)
     for u in range(views):
         for w in range(views):
             pairs[count] = u * views + w
-            count = count + (view_set[u] == view_set[w]).astype(jnp.int32)
+            count = count + (view_set[u] == key_set(w)).astype(jnp.int32)
     for w in range(views):
-        k_rows = slice((w % here) * HEAD_DIM, (w % here + 1) * HEAD_DIM)
-        v_rows = slice((here + w % here) * HEAD_DIM, (here + w % here + 1) * HEAD_DIM)
+        base = (w // here * 2 * here + w % here) * HEAD_DIM
         for p in range(patches):
             at = (w * patches + p) * tok
-            store_keys(keys, at, packed[(w // here) * patches + p, k_rows, :])
-            values[0:HEAD_DIM, at : at + tok] = packed[(w // here) * patches + p, v_rows, :]
+            store_keys(keys, at, packed[p, base : base + HEAD_DIM, :])
+            value_base = base + here * HEAD_DIM
+            values[0:HEAD_DIM, at : at + tok] = packed[p, value_base : value_base + HEAD_DIM, :]
     values[HEAD_DIM:, :] = jnp.ones((VALUE_ROWS - HEAD_DIM, views * span), BF16)
     sums[...] = jnp.zeros(sums.shape, F32)
 
@@ -332,7 +344,7 @@
             )
 
             def look(w, top):
-                seen = jnp.where(view_set[u] == view_set[w], span, 0)
+                seen = jnp.where(view_set[u] == key_set(w), span, 0)
                 return block_max(keys, w * span, seen, tok, plain, top)
 
             top = lax.fori_loop(0, views, look, old)
@@ -342,7 +354,7 @@
 
             @pl.loop(0, views)
             def _(w):
-                @pl.when(view_set[u] == view_set[w])
+                @pl.when(view_set[u] == key_set(w))
                 def _():
                     @pl.loop(0, patches)
                     def _(p):
@@ -357,20 +369,21 @@
             out[(u // here) * patches + p, rows, :] = context[:, p * tok : (p + 1) * tok]
 
 
-def generated_part(view_set, query, before, packed):
-    sources, rows, tok = packed.shape
+def generated_part(view_set, view, query, before, packed):
+    patches, rows, tok = packed.shape
     views, _, span = query.shape
     vmem = pl.BlockSpec(memory_space=pltpu.VMEM)
     return pl.pallas_call(
         generated_kernel,
         in_specs=[
             pl.BlockSpec(memory_space=pltpu.SMEM),
+            pl.BlockSpec(memory_space=pltpu.SMEM),
             vmem,
             pl.BlockSpec(memory_space=pltpu.MemorySpace.HBM),
             vmem,
         ],
         out_specs=vmem,
-        out_shape=jax.ShapeDtypeStruct((sources, rows // 2, tok), BF16),
+        out_shape=jax.ShapeDtypeStruct((2 * patches, rows // 4, tok), BF16),
         scratch_shapes=[
             pltpu.VMEM((views * span, KEY_COLS), BF16),
             pltpu.VMEM((VALUE_ROWS, views * span), BF16),
@@ -382,7 +395,7 @@
         compiler_params=params(32),
         cost_estimate=cost(6 * views * views * span * span * HEAD_DIM, 4 * MIB),
         name="generated_part",
-    )(view_set, query, pltpu.with_memory_space_constraint(before, pltpu.MemorySpace.HBM), packed)
+    )(view_set, view, query, pltpu.with_memory_space_constraint(before, pltpu.MemorySpace.HBM), packed)
 
 
 def project_out_kernel(packed, weight, out, context, blocks, sems):
@@ -430,9 +443,12 @@
     views = view_set.shape[0]
     view = lax.axis_index("view").astype(jnp.int32).reshape(1)
     queries = exchange(pack_queries(view, hidden, rays, w_query, obs_keys, obs_values))
-    pairs = exchange(pack_pairs(hidden, rays, w_key, w_value))
+    keep, give = pack_pairs(view, hidden, rays, w_key, w_value)
+    got = lax.ppermute(give, "view", [(0, 1), (1, 0)])
+    pairs = jnp.concatenate([keep, got], axis=1)
+    pairs = lax.all_to_all(pairs, "patch", split_axis=0, concat_axis=0, tiled=True)
     query, before = observed_part(queries, views, obs_keys.shape[0])
-    context = exchange(generated_part(view_set, query, before, pairs))
+    context = exchange(generated_part(view_set, view, query, before, pairs))
     return project_out(context, w_out)
 
 

time: 180 us -> 180 us (level)
  the two profiles are of different devices: /device:TPU:6 before, /device:TPU:27 now
where the time goes in v4:
time: 180 us
  Pallas kernels  79.6 us (44%)
  blocking collectives  75 us (42%)
  waiting for transfers between devices  11.7 us (6%)
  starting transfers between devices  11.3 us (6%)
  other arithmetic  2.09 us (1%)
    all_to_all x1, blocking collectives, exchange(): lax.all_to_all(blocks, ('view', 'patch'), split_axis=0, concat_axis=0, ti...  75 us
    pallas_call x1, Pallas kernels, generated_part(): pl.pallas_call(generated_kernel, in_specs=[pl.BlockSpec(memory_space=pltp...  57.3 us
    pallas_call x1, Pallas kernels, observed_part(): pl.pallas_call(observed_kernel, in_specs=[vmem], out_specs=[vmem, pl.Bloc...  12.7 us
    all_to_all x1, waiting for transfers between devices, exchange(): lax.all_to_all(blocks, ('view', 'patch'), split_axis=0, concat_axis=0, ti...  8.67 us
    all_to_all x1, starting transfers between devices, exchange(): lax.all_to_all(blocks, ('view', 'patch'), split_axis=0, concat_axis=0, ti...  7.11 us
    pallas_call x1, Pallas kernels, pack_pairs(): pl.pallas_call(pack_pairs_kernel, in_specs=[pl.BlockSpec(memory_space=plt...  4.63 us
    all_to_all x1, starting transfers between devices, on_device(): lax.all_to_all(pairs, 'patch', split_axis=0, concat_axis=0, tiled=True)  3.74 us
  transfers between devices with their start and end apart: 3, of which 3 were waited for; matrix products, arithmetic and copies ran while one was open for 1% of the time, Pallas kernels for 10%

profile of v4, /device:TPU:27, one launch (start us, length us, event | category | flops | bytes accessed | tf_op | source)
XLA Modules:
  0.0 179.7 jit_solution(17304821032528289197)
XLA Ops:
  0.0 3.6 %pack_queries.1 = bf16[16,320,128]{2,1,0:T(8,128)(2,1)} custom-call(s32[1]{0:T(128)} %bitcast.view, bf16[2,128,1024]{2,1,0:T(8,128)(2,1)} %hidden.3, bf16[2,128,1024]{2,1,0:T(8,128)(2,1)} %rays.3, bf16[1024,1024]{1,0:T(8,128)(2,1)} %weight.2, bf16[3,128,1024]{2,1,0:T(8,128)(2,1)} %obs_k.1, bf16[3,128,1024]{2,1,0:T(8,128)(2,1)} %obs_v.1), custom_call_target="tpu_custom_call" | custom-call | flops 536870912 | bytes 6291456 | tf_op jit(solution)/shard_map/pack_queries/pallas_call | solution.py:100
  3.6 7.1 %all-to-all-start = ((bf16[16,320,128]{2,1,0:T(8,128)(2,1)}), bf16[16,320,128]{2,1,0:T(8,128)(2,1)S(1)}, u32[]{:S(2)}, u32[]{:S(2)}) async-start(bf16[16,320,128]{2,1,0:T(8,128)(2,1)} %pack_queries.1), calls=%async_computation | async-start | bytes 2621440 | tf_op jit(solution)/shard_map/all_to_all | solution.py:439
  10.7 4.6 %pack_pairs.1 = (bf16[8,256,128]{2,1,0:T(8,128)(2,1)}, bf16[8,256,128]{2,1,0:T(8,128)(2,1)}) custom-call(s32[1]{0:T(128)} %bitcast.view, bf16[2,128,1024]{2,1,0:T(8,128)(2,1)} %hidden.3, bf16[2,128,1024]{2,1,0:T(8,128)(2,1)} %rays.3, bf16[1024,1024]{1,0:T(8,128)(2,1)} %w_key.1, bf16[1024,1024]{1,0:T(8,128)(2,1)} %w_value.1), custom_call_target="tpu_custom_call" | custom-call | flops 1073741824 | bytes 7340032 | tf_op jit(solution)/shard_map/pack_pairs/pallas_call | solution.py:153
  15.3 0.4 collective-permute-start
  15.8 1.8 collective-permute-done
  17.5 2.1 %pad_maximum_fusion = bf16[8,512,128]{2,1,0:T(8,128)(2,1)} fusion(bf16[8,256,128]{2,1,0:T(8,128)(2,1)S(1)} %collective-permute-done, bf16[8,256,128]{2,1,0:T(8,128)(2,1)} %get-tuple-element.11), kind=kLoop, calls=%fused_computation | loop fusion | flops 2097152 | bytes 2097152 | tf_op jit(solution)/shard_map/concatenate | solution.py:448
  19.6 8.7 %all-to-all-done.packed = bf16[16,320,128]{2,1,0:T(8,128)(2,1)S(1)} async-done(((bf16[16,320,128]{2,1,0:T(8,128)(2,1)}), bf16[16,320,128]{2,1,0:T(8,128)(2,1)S(1)}, u32[]{:S(2)}, u32[]{:S(2)}) %all-to-all-start) | async-done | bytes 1310752 | tf_op jit(solution)/shard_map/all_to_all | solution.py:439
  28.3 3.7 %all-to-all-start.1 = ((bf16[8,512,128]{2,1,0:T(8,128)(2,1)}), bf16[8,512,128]{2,1,0:T(8,128)(2,1)S(1)}, u32[]{:S(2)}, u32[]{:S(2)}) async-start(bf16[8,512,128]{2,1,0:T(8,128)(2,1)} %pad_maximum_fusion), calls=%async_computation.1 | async-start | bytes 2097152 | tf_op jit(solution)/shard_map/all_to_all | solution.py:449
  32.0 0.0 copy-start.1
  32.0 12.7 %observed_part.1 = (bf16[4,128,1024]{2,1,0:T(8,128)(2,1)S(1)}, f32[4,80,1024]{2,1,0:T(8,128)}) custom-call(bf16[16,320,128]{2,1,0:T(8,128)(2,1)S(1)} %all-to-all-done.packed), custom_call_target="tpu_custom_call" | custom-call | flops 6442450944 | bytes 4194304 | tf_op jit(solution)/shard_map/observed_part/pallas_call | solution.py:274
  44.7 1.3 all-to-all-done.1.packed
  46.0 0.0 copy-done.1
  46.0 0.0 copy-start
  46.0 57.3 %generated_part.1 = bf16[16,128,128]{2,1,0:T(8,128)(2,1)S(1)} custom-call(s32[4]{0:T(128)S(1)} %copy-done.1, s32[1]{0:T(128)} %bitcast.view, bf16[4,128,1024]{2,1,0:T(8,128)(2,1)S(1)} %get-tuple-element.9.query, f32[4,80,1024]{2,1,0:T(8,128)} %get-tuple-element.10.before, bf16[8,512,128]{2,1,0:T(8,128)(2,1)S(1)} %all-to-all-done.1.packed), custom_call_target="tpu_custom_call" | custom-call | flops 6442450944 | bytes 4194304 | tf_op jit(solution)/shard_map/generated_part/pallas_call | solution.py:376
  103.3 75.0 %all_to_all.15.packed = bf16[16,128,128]{2,1,0:T(8,128)(2,1)S(1)} all-to-all(bf16[16,128,128]{2,1,0:T(8,128)(2,1)S(1)} %generated_part.1), channel_id=1, replica_groups=mesh['group'=8,'view'=2,'patch'=8] {'view','patch'}, dimensions={0} | all-to-all | bytes 1048576 | tf_op jit(solution)/shard_map/all_to_all | solution.py:439
  178.3 0.0 copy-done
  178.3 1.5 project_out.1
Async XLA Ops:
  3.6 24.7 %all-to-all-start = ((bf16[16,320,128]{2,1,0:T(8,128)(2,1)}), bf16[16,320,128]{2,1,0:T(8,128)(2,1)S(1)}, u32[]{:S(2)}, u32[]{:S(2)}) async-start(bf16[16,320,128]{2,1,0:T(8,128)(2,1)} %pack_queries.1), calls=%async_computation | async-start | bytes 2621440 | tf_op jit(solution)/shard_map/all_to_all | solution.py:439
  15.3 2.2 %collective-permute-start = (bf16[8,256,128]{2,1,0:T(8,128)(2,1)}, bf16[8,256,128]{2,1,0:T(8,128)(2,1)S(1)}, u32[]{:S(2)}, u32[]{:S(2)}) collective-permute-start(bf16[8,256,128]{2,1,0:T(8,128)(2,1)} %get-tuple-element.12), channel_id=1, source_target_pairs={{0,8},{8,0},{1,9},{9,1},{2,10},{10,2},{3,11},{11,3},{4,12},{12,4},... | collective-permute-start | bytes 1572872 | tf_op jit(solution)/shard_map/ppermute | solution.py:447
  28.3 17.7 %all-to-all-start.1 = ((bf16[8,512,128]{2,1,0:T(8,128)(2,1)}), bf16[8,512,128]{2,1,0:T(8,128)(2,1)S(1)}, u32[]{:S(2)}, u32[]{:S(2)}) async-start(bf16[8,512,128]{2,1,0:T(8,128)(2,1)} %pad_maximum_fusion), calls=%async_computation.1 | async-start | bytes 2097152 | tf_op jit(solution)/shard_map/all_to_all | solution.py:449
  32.0 14.0 %copy-start.1 = (s32[4]{0:T(128)S(1)}, s32[4]{0:T(128)}, u32[]{:S(2)}) copy-start(s32[4]{0:T(128)} %view_set.1) | copy-start | bytes 52
  46.0 132.2 %copy-start = (bf16[1024,1024]{1,0:T(8,128)(2,1)S(1)}, bf16[1024,1024]{1,0:T(8,128)(2,1)}, u32[]{:S(2)}) copy-start(bf16[1024,1024]{1,0:T(8,128)(2,1)} %weight.3) | copy-start | bytes 6291460

commit v5 on v4

--- a/solution.py
+++ b/solution.py
@@ -323,12 +323,21 @@
         start = pl.multiple_of((pairs[i] % views) * span, span)
         return u, weighted(keys, values, start, span, query[u])
 
-    @pl.loop(0, count // 2)
-    def _(i):
-        u0, term0 = one_pair(2 * i)
-        u1, term1 = one_pair(2 * i + 1)
-        sums[u0] += term0
-        sums[u1] += term1
+    def several(first, width):
+        for u, term in [one_pair(first + i) for i in range(width)]:
+            sums[u] += term
+
+    @pl.when(count % 5 == 0)
+    def _():
+        @pl.loop(0, count // 5)
+        def _(i):
+            several(5 * i, 5)
+
+    @pl.when(count % 5 != 0)
+    def _():
+        @pl.loop(0, count // 4)
+        def _(i):
+            several(4 * i, 4)
 
     largest = jnp.max(sums[:, SUM_ROW : SUM_ROW + 1, :])
     fetch.wait()
@@ -363,7 +372,7 @@
 
     for u in range(views):
         total = sums[u] + early[u]
-        context = (total[0:HEAD_DIM] / total[SUM_ROW : SUM_ROW + 1]).astype(BF16)
+        context = (total[0:HEAD_DIM] * (1.0 / total[SUM_ROW : SUM_ROW + 1])).astype(BF16)
         rows = slice((u % here) * HEAD_DIM, (u % here + 1) * HEAD_DIM)
         for p in range(patches):
             out[(u // here) * patches + p, rows, :] = context[:, p * tok : (p + 1) * tok]

time: 180 us -> 180 us (level)
  Pallas kernels: 79.6 us -> 140 us
  blocking collectives: 75 us -> 15.7 us
    pallas_call x1, Pallas kernels: 12.7 us -> 73.2 us  [observed_part(): pl.pallas_call(observed_kernel, in_specs=[vmem], out_specs=[vmem, pl.Bloc...]
    all_to_all x1, blocking collectives: 75 us -> 15.7 us  [exchange(): lax.all_to_all(blocks, ('view', 'patch'), split_axis=0, concat_axis=0, ti...]
  transfers between devices with their start and end apart: 3 -> 3, of which waited for: 3 -> 2; matrix products, arithmetic and copies ran while one was open for 1% -> 1% of each run, Pallas kernels for 10% -> 43%
where the time goes in v5:
time: 180 us
  Pallas kernels  140 us (78%)
  blocking collectives  15.7 us (9%)
  starting transfers between devices  11.3 us (6%)
  waiting for transfers between devices  10.4 us (6%)
  other arithmetic  2.09 us (1%)
    pallas_call x1, Pallas kernels, observed_part(): pl.pallas_call(observed_kernel, in_specs=[vmem], out_specs=[vmem, pl.Bloc...  73.2 us
    pallas_call x1, Pallas kernels, generated_part(): pl.pallas_call(generated_kernel, in_specs=[pl.BlockSpec(memory_space=pltp...  57.1 us
    all_to_all x1, blocking collectives, exchange(): lax.all_to_all(blocks, ('view', 'patch'), split_axis=0, concat_axis=0, ti...  15.7 us
    all_to_all x1, waiting for transfers between devices, exchange(): lax.all_to_all(blocks, ('view', 'patch'), split_axis=0, concat_axis=0, ti...  8.67 us
    all_to_all x1, starting transfers between devices, exchange(): lax.all_to_all(blocks, ('view', 'patch'), split_axis=0, concat_axis=0, ti...  7.11 us
    pallas_call x1, Pallas kernels, pack_pairs(): pl.pallas_call(pack_pairs_kernel, in_specs=[pl.BlockSpec(memory_space=plt...  4.63 us
    all_to_all x1, starting transfers between devices, on_device(): lax.all_to_all(pairs, 'patch', split_axis=0, concat_axis=0, tiled=True)  3.74 us
  transfers between devices with their start and end apart: 3, of which 2 were waited for; matrix products, arithmetic and copies ran while one was open for 1% of the time, Pallas kernels for 43%

profile of v5, /device:TPU:27, one launch (start us, length us, event | category | flops | bytes accessed | tf_op | source)
XLA Modules:
  0.0 179.7 jit_solution(5429718039223356157)
XLA Ops:
  0.0 3.6 %pack_queries.1 = bf16[16,320,128]{2,1,0:T(8,128)(2,1)} custom-call(s32[1]{0:T(128)} %bitcast.view, bf16[2,128,1024]{2,1,0:T(8,128)(2,1)} %hidden.3, bf16[2,128,1024]{2,1,0:T(8,128)(2,1)} %rays.3, bf16[1024,1024]{1,0:T(8,128)(2,1)} %weight.2, bf16[3,128,1024]{2,1,0:T(8,128)(2,1)} %obs_k.1, bf16[3,128,1024]{2,1,0:T(8,128)(2,1)} %obs_v.1), custom_call_target="tpu_custom_call" | custom-call | flops 536870912 | bytes 6291456 | tf_op jit(solution)/shard_map/pack_queries/pallas_call | solution.py:100
  3.6 7.1 %all-to-all-start = ((bf16[16,320,128]{2,1,0:T(8,128)(2,1)}), bf16[16,320,128]{2,1,0:T(8,128)(2,1)S(1)}, u32[]{:S(2)}, u32[]{:S(2)}) async-start(bf16[16,320,128]{2,1,0:T(8,128)(2,1)} %pack_queries.1), calls=%async_computation | async-start | bytes 2621440 | tf_op jit(solution)/shard_map/all_to_all | solution.py:448
  10.7 4.6 %pack_pairs.1 = (bf16[8,256,128]{2,1,0:T(8,128)(2,1)}, bf16[8,256,128]{2,1,0:T(8,128)(2,1)}) custom-call(s32[1]{0:T(128)} %bitcast.view, bf16[2,128,1024]{2,1,0:T(8,128)(2,1)} %hidden.3, bf16[2,128,1024]{2,1,0:T(8,128)(2,1)} %rays.3, bf16[1024,1024]{1,0:T(8,128)(2,1)} %w_key.1, bf16[1024,1024]{1,0:T(8,128)(2,1)} %w_value.1), custom_call_target="tpu_custom_call" | custom-call | flops 1073741824 | bytes 7340032 | tf_op jit(solution)/shard_map/pack_pairs/pallas_call | solution.py:153
  15.3 0.4 collective-permute-start
  15.8 1.8 collective-permute-done
  17.5 2.1 %pad_maximum_fusion = bf16[8,512,128]{2,1,0:T(8,128)(2,1)} fusion(bf16[8,256,128]{2,1,0:T(8,128)(2,1)S(1)} %collective-permute-done, bf16[8,256,128]{2,1,0:T(8,128)(2,1)} %get-tuple-element.11), kind=kLoop, calls=%fused_computation | loop fusion | flops 2097152 | bytes 2097152 | tf_op jit(solution)/shard_map/concatenate | solution.py:457
  19.6 8.7 %all-to-all-done.packed = bf16[16,320,128]{2,1,0:T(8,128)(2,1)S(1)} async-done(((bf16[16,320,128]{2,1,0:T(8,128)(2,1)}), bf16[16,320,128]{2,1,0:T(8,128)(2,1)S(1)}, u32[]{:S(2)}, u32[]{:S(2)}) %all-to-all-start) | async-done | bytes 1310752 | tf_op jit(solution)/shard_map/all_to_all | solution.py:448
  28.3 3.7 %all-to-all-start.1 = ((bf16[8,512,128]{2,1,0:T(8,128)(2,1)}), bf16[8,512,128]{2,1,0:T(8,128)(2,1)S(1)}, u32[]{:S(2)}, u32[]{:S(2)}) async-start(bf16[8,512,128]{2,1,0:T(8,128)(2,1)} %pad_maximum_fusion), calls=%async_computation.1 | async-start | bytes 2097152 | tf_op jit(solution)/shard_map/all_to_all | solution.py:458
  32.0 0.0 copy-start.1
  32.0 73.2 %observed_part.1 = (bf16[4,128,1024]{2,1,0:T(8,128)(2,1)S(1)}, f32[4,80,1024]{2,1,0:T(8,128)}) custom-call(bf16[16,320,128]{2,1,0:T(8,128)(2,1)S(1)} %all-to-all-done.packed), custom_call_target="tpu_custom_call" | custom-call | flops 6442450944 | bytes 4194304 | tf_op jit(solution)/shard_map/observed_part/pallas_call | solution.py:274
  105.2 0.0 all-to-all-done.1.packed
  105.2 0.0 copy-done.1
  105.2 0.0 copy-start
  105.2 57.1 %generated_part.1 = bf16[16,128,128]{2,1,0:T(8,128)(2,1)S(1)} custom-call(s32[4]{0:T(128)S(1)} %copy-done.1, s32[1]{0:T(128)} %bitcast.view, bf16[4,128,1024]{2,1,0:T(8,128)(2,1)S(1)} %get-tuple-element.9.query, f32[4,80,1024]{2,1,0:T(8,128)} %get-tuple-element.10.before, bf16[8,512,128]{2,1,0:T(8,128)(2,1)S(1)} %all-to-all-done.1.packed), custom_call_target="tpu_custom_call" | custom-call | flops 6442450944 | bytes 4194304 | tf_op jit(solution)/shard_map/generated_part/pallas_call | solution.py:385
  162.3 15.7 %all_to_all.15.packed = bf16[16,128,128]{2,1,0:T(8,128)(2,1)S(1)} all-to-all(bf16[16,128,128]{2,1,0:T(8,128)(2,1)S(1)} %generated_part.1), channel_id=1, replica_groups=mesh['group'=8,'view'=2,'patch'=8] {'view','patch'}, dimensions={0} | all-to-all | bytes 1048576 | tf_op jit(solution)/shard_map/all_to_all | solution.py:448
  178.0 0.0 copy-done
  178.0 1.5 project_out.1
Async XLA Ops:
  3.6 24.7 %all-to-all-start = ((bf16[16,320,128]{2,1,0:T(8,128)(2,1)}), bf16[16,320,128]{2,1,0:T(8,128)(2,1)S(1)}, u32[]{:S(2)}, u32[]{:S(2)}) async-start(bf16[16,320,128]{2,1,0:T(8,128)(2,1)} %pack_queries.1), calls=%async_computation | async-start | bytes 2621440 | tf_op jit(solution)/shard_map/all_to_all | solution.py:448
  15.3 2.2 %collective-permute-start = (bf16[8,256,128]{2,1,0:T(8,128)(2,1)}, bf16[8,256,128]{2,1,0:T(8,128)(2,1)S(1)}, u32[]{:S(2)}, u32[]{:S(2)}) collective-permute-start(bf16[8,256,128]{2,1,0:T(8,128)(2,1)} %get-tuple-element.12), channel_id=1, source_target_pairs={{0,8},{8,0},{1,9},{9,1},{2,10},{10,2},{3,11},{11,3},{4,12},{12,4},... | collective-permute-start | bytes 1572872 | tf_op jit(solution)/shard_map/ppermute | solution.py:456
  28.3 76.9 %all-to-all-start.1 = ((bf16[8,512,128]{2,1,0:T(8,128)(2,1)}), bf16[8,512,128]{2,1,0:T(8,128)(2,1)S(1)}, u32[]{:S(2)}, u32[]{:S(2)}) async-start(bf16[8,512,128]{2,1,0:T(8,128)(2,1)} %pad_maximum_fusion), calls=%async_computation.1 | async-start | bytes 2097152 | tf_op jit(solution)/shard_map/all_to_all | solution.py:458
  32.0 73.2 %copy-start.1 = (s32[4]{0:T(128)S(1)}, s32[4]{0:T(128)}, u32[]{:S(2)}) copy-start(s32[4]{0:T(128)} %view_set.1) | copy-start | bytes 52
  105.2 72.8 %copy-start = (bf16[1024,1024]{1,0:T(8,128)(2,1)S(1)}, bf16[1024,1024]{1,0:T(8,128)(2,1)}, u32[]{:S(2)}) copy-start(bf16[1024,1024]{1,0:T(8,128)(2,1)} %weight.3) | copy-start | bytes 6291460

commit v6 on v5

--- a/solution.py
+++ b/solution.py
@@ -29,6 +29,7 @@
 
 
 HBM = pl.BlockSpec(memory_space=pltpu.MemorySpace.HBM)
+PATCHES = (0, 3, 2, 5, 4, 7, 6, 1)
 COLUMNS = 2
 
 
@@ -47,12 +48,15 @@
     source[...] = both.astype(BF16).reshape(source.shape)
 
 
-def place(blocks, first, base, feats, count, tok):
+def place(blocks, first, base, feats, count, tok, order=None):
     for head in range(feats.shape[0] // HEAD_DIM):
+        to = first + head
+        if order:
+            to = to // len(order) * len(order) + order.index(to % len(order))
         rows = slice(head * HEAD_DIM, (head + 1) * HEAD_DIM)
         for i in range(count):
             at = (base + i) * HEAD_DIM
-            blocks[first + head, at : at + HEAD_DIM, :] = feats[rows, i * tok : (i + 1) * tok]
+            blocks[to, at : at + HEAD_DIM, :] = feats[rows, i * tok : (i + 1) * tok]
 
 
 def pack_queries_kernel(
@@ -135,7 +139,7 @@
         for j in range(COLUMNS):
             columns[i * COLUMNS + j].wait()
             feats = dot(source[...], held[:, j * cols : (j + 1) * cols]).astype(BF16)
-            place(blocks, j * heads, i * views, feats.T, views, tok)
+            place(blocks, j * heads, i * views, feats.T, views, tok, PATCHES)
     half = keep.shape[0]
     sends = [
         pltpu.make_async_copy(blocks.at[pl.ds(side * half, half)], out, out_sem.at[i])
@@ -240,10 +244,11 @@
     def send(u):
         return pltpu.make_async_copy(sums.at[u], sums_out.at[u], sems.at[u])
 
-    @pl.loop(0, views)
-    def _(u):
-        one_view(u, span)
-        send(u).start()
+    @pl.loop(0, views // 2)
+    def _(i):
+        for u in (2 * i, 2 * i + 1):
+            one_view(u, span)
+            send(u).start()
 
     largest = jnp.max(sums[:, SUM_ROW : SUM_ROW + 1, :])
     for u in range(views):
@@ -455,7 +460,9 @@
     keep, give = pack_pairs(view, hidden, rays, w_key, w_value)
     got = lax.ppermute(give, "view", [(0, 1), (1, 0)])
     pairs = jnp.concatenate([keep, got], axis=1)
-    pairs = lax.all_to_all(pairs, "patch", split_axis=0, concat_axis=0, tiled=True)
+    pairs = lax.all_to_all(
+        pairs, "patch", split_axis=0, concat_axis=0, tiled=True, axis_index_groups=[list(PATCHES)]
+    )
     query, before = observed_part(queries, views, obs_keys.shape[0])
     context = exchange(generated_part(view_set, view, query, before, pairs))
     return project_out(context, w_out)

time: 180 us -> 180 us (level)
  no operation moved by 1% of the time
where the time goes in v6:
time: 180 us
  Pallas kernels  140 us (78%)
  blocking collectives  15.6 us (9%)
  starting transfers between devices  11.3 us (6%)
  waiting for transfers between devices  10.4 us (6%)
  other arithmetic  2.09 us (1%)
    pallas_call x1, Pallas kernels, observed_part(): pl.pallas_call(observed_kernel, in_specs=[vmem], out_specs=[vmem, pl.Bloc...  72.9 us
    pallas_call x1, Pallas kernels, generated_part(): pl.pallas_call(generated_kernel, in_specs=[pl.BlockSpec(memory_space=pltp...  57.3 us
    all_to_all x1, blocking collectives, exchange(): lax.all_to_all(blocks, ('view', 'patch'), split_axis=0, concat_axis=0, ti...  15.6 us
    all_to_all x1, waiting for transfers between devices, exchange(): lax.all_to_all(blocks, ('view', 'patch'), split_axis=0, concat_axis=0, ti...  8.67 us
    all_to_all x1, starting transfers between devices, exchange(): lax.all_to_all(blocks, ('view', 'patch'), split_axis=0, concat_axis=0, ti...  7.11 us
    pallas_call x1, Pallas kernels, pack_pairs(): pl.pallas_call(pack_pairs_kernel, in_specs=[pl.BlockSpec(memory_space=plt...  4.63 us
    all_to_all x1, starting transfers between devices, on_device(): lax.all_to_all(pairs, 'patch', split_axis=0, concat_axis=0, tiled=True, a...  3.78 us
  transfers between devices with their start and end apart: 3, of which 2 were waited for; matrix products, arithmetic and copies ran while one was open for 1% of the time, Pallas kernels for 43%

profile of v6, /device:TPU:27, one launch (start us, length us, event | category | flops | bytes accessed | tf_op | source)
XLA Modules:
  0.0 179.6 jit_solution(10336437983588061349)
XLA Ops:
  0.0 3.6 %pack_queries.1 = bf16[16,320,128]{2,1,0:T(8,128)(2,1)} custom-call(s32[1]{0:T(128)} %bitcast.view, bf16[2,128,1024]{2,1,0:T(8,128)(2,1)} %hidden.3, bf16[2,128,1024]{2,1,0:T(8,128)(2,1)} %rays.3, bf16[1024,1024]{1,0:T(8,128)(2,1)} %weight.2, bf16[3,128,1024]{2,1,0:T(8,128)(2,1)} %obs_k.1, bf16[3,128,1024]{2,1,0:T(8,128)(2,1)} %obs_v.1), custom_call_target="tpu_custom_call" | custom-call | flops 536870912 | bytes 6291456 | tf_op jit(solution)/shard_map/pack_queries/pallas_call | solution.py:104
  3.6 7.1 %all-to-all-start = ((bf16[16,320,128]{2,1,0:T(8,128)(2,1)}), bf16[16,320,128]{2,1,0:T(8,128)(2,1)S(1)}, u32[]{:S(2)}, u32[]{:S(2)}) async-start(bf16[16,320,128]{2,1,0:T(8,128)(2,1)} %pack_queries.1), calls=%async_computation | async-start | bytes 2621440 | tf_op jit(solution)/shard_map/all_to_all | solution.py:453
  10.7 4.6 %pack_pairs.1 = (bf16[8,256,128]{2,1,0:T(8,128)(2,1)}, bf16[8,256,128]{2,1,0:T(8,128)(2,1)}) custom-call(s32[1]{0:T(128)} %bitcast.view, bf16[2,128,1024]{2,1,0:T(8,128)(2,1)} %hidden.3, bf16[2,128,1024]{2,1,0:T(8,128)(2,1)} %rays.3, bf16[1024,1024]{1,0:T(8,128)(2,1)} %w_key.1, bf16[1024,1024]{1,0:T(8,128)(2,1)} %w_value.1), custom_call_target="tpu_custom_call" | custom-call | flops 1073741824 | bytes 7340032 | tf_op jit(solution)/shard_map/pack_pairs/pallas_call | solution.py:157
  15.3 0.4 collective-permute-start
  15.8 1.8 collective-permute-done
  17.5 2.1 %pad_maximum_fusion = bf16[8,512,128]{2,1,0:T(8,128)(2,1)} fusion(bf16[8,256,128]{2,1,0:T(8,128)(2,1)S(1)} %collective-permute-done, bf16[8,256,128]{2,1,0:T(8,128)(2,1)} %get-tuple-element.11), kind=kLoop, calls=%fused_computation | loop fusion | flops 2097152 | bytes 2097152 | tf_op jit(solution)/shard_map/concatenate | solution.py:462
  19.6 8.7 %all-to-all-done.packed = bf16[16,320,128]{2,1,0:T(8,128)(2,1)S(1)} async-done(((bf16[16,320,128]{2,1,0:T(8,128)(2,1)}), bf16[16,320,128]{2,1,0:T(8,128)(2,1)S(1)}, u32[]{:S(2)}, u32[]{:S(2)}) %all-to-all-start) | async-done | bytes 1310752 | tf_op jit(solution)/shard_map/all_to_all | solution.py:453
  28.3 3.8 %all-to-all-start.1 = ((bf16[8,512,128]{2,1,0:T(8,128)(2,1)}), bf16[8,512,128]{2,1,0:T(8,128)(2,1)S(1)}, u32[]{:S(2)}, u32[]{:S(2)}) async-start(bf16[8,512,128]{2,1,0:T(8,128)(2,1)} %pad_maximum_fusion), calls=%async_computation.1 | async-start | bytes 2097152 | tf_op jit(solution)/shard_map/all_to_all | solution.py:463
  32.1 0.0 copy-start.1
  32.1 72.9 %observed_part.1 = (bf16[4,128,1024]{2,1,0:T(8,128)(2,1)S(1)}, f32[4,80,1024]{2,1,0:T(8,128)}) custom-call(bf16[16,320,128]{2,1,0:T(8,128)(2,1)S(1)} %all-to-all-done.packed), custom_call_target="tpu_custom_call" | custom-call | flops 6442450944 | bytes 4194304 | tf_op jit(solution)/shard_map/observed_part/pallas_call | solution.py:279
  105.0 0.0 all-to-all-done.1.packed
  105.0 0.0 copy-done.1
  105.0 0.0 copy-start
  105.0 57.3 %generated_part.1 = bf16[16,128,128]{2,1,0:T(8,128)(2,1)S(1)} custom-call(s32[4]{0:T(128)S(1)} %copy-done.1, s32[1]{0:T(128)} %bitcast.view, bf16[4,128,1024]{2,1,0:T(8,128)(2,1)S(1)} %get-tuple-element.9.query, f32[4,80,1024]{2,1,0:T(8,128)} %get-tuple-element.10.before, bf16[8,512,128]{2,1,0:T(8,128)(2,1)S(1)} %all-to-all-done.1.packed), custom_call_target="tpu_custom_call" | custom-call | flops 6442450944 | bytes 4194304 | tf_op jit(solution)/shard_map/generated_part/pallas_call | solution.py:390
  162.3 15.6 %all_to_all.15.packed = bf16[16,128,128]{2,1,0:T(8,128)(2,1)S(1)} all-to-all(bf16[16,128,128]{2,1,0:T(8,128)(2,1)S(1)} %generated_part.1), channel_id=1, replica_groups=mesh['group'=8,'view'=2,'patch'=8] {'view','patch'}, dimensions={0} | all-to-all | bytes 1048576 | tf_op jit(solution)/shard_map/all_to_all | solution.py:453
  177.9 0.0 copy-done
  177.9 1.5 project_out.1
Async XLA Ops:
  3.6 24.7 %all-to-all-start = ((bf16[16,320,128]{2,1,0:T(8,128)(2,1)}), bf16[16,320,128]{2,1,0:T(8,128)(2,1)S(1)}, u32[]{:S(2)}, u32[]{:S(2)}) async-start(bf16[16,320,128]{2,1,0:T(8,128)(2,1)} %pack_queries.1), calls=%async_computation | async-start | bytes 2621440 | tf_op jit(solution)/shard_map/all_to_all | solution.py:453
  15.3 2.2 %collective-permute-start = (bf16[8,256,128]{2,1,0:T(8,128)(2,1)}, bf16[8,256,128]{2,1,0:T(8,128)(2,1)S(1)}, u32[]{:S(2)}, u32[]{:S(2)}) collective-permute-start(bf16[8,256,128]{2,1,0:T(8,128)(2,1)} %get-tuple-element.12), channel_id=1, source_target_pairs={{0,8},{8,0},{1,9},{9,1},{2,10},{10,2},{3,11},{11,3},{4,12},{12,4},... | collective-permute-start | bytes 1572872 | tf_op jit(solution)/shard_map/ppermute | solution.py:461
  28.3 76.7 %all-to-all-start.1 = ((bf16[8,512,128]{2,1,0:T(8,128)(2,1)}), bf16[8,512,128]{2,1,0:T(8,128)(2,1)S(1)}, u32[]{:S(2)}, u32[]{:S(2)}) async-start(bf16[8,512,128]{2,1,0:T(8,128)(2,1)} %pad_maximum_fusion), calls=%async_computation.1 | async-start | bytes 2097152 | tf_op jit(solution)/shard_map/all_to_all | solution.py:463
  32.1 72.9 %copy-start.1 = (s32[4]{0:T(128)S(1)}, s32[4]{0:T(128)}, u32[]{:S(2)}) copy-start(s32[4]{0:T(128)} %view_set.1) | copy-start | bytes 52
  105.0 73.0 %copy-start = (bf16[1024,1024]{1,0:T(8,128)(2,1)S(1)}, bf16[1024,1024]{1,0:T(8,128)(2,1)}, u32[]{:S(2)}) copy-start(bf16[1024,1024]{1,0:T(8,128)(2,1)} %weight.3) | copy-start | bytes 6291460

commit v7 on v5

--- a/solution.py
+++ b/solution.py
@@ -10,6 +10,7 @@
 SUM_ROW = HEAD_DIM
 VALUE_ROWS = HEAD_DIM + 16
 KEY_COLS = 2 * HEAD_DIM
+FIRST_KEYS = 32
 LIMIT = 2.0**100
 BF16 = jnp.bfloat16
 F32 = jnp.float32
@@ -226,7 +227,7 @@
         rows = slice((u % here) * HEAD_DIM, (u % here + 1) * HEAD_DIM)
         query = jnp.concatenate([packed[(u // here) * patches + p, rows, :] for p in range(patches)], axis=1)
         query_out[u, 0:HEAD_DIM, :] = query
-        top = jnp.max(dot(keys[0:tok, 0:HEAD_DIM], query), axis=0, keepdims=True)
+        top = jnp.max(dot(keys[0:FIRST_KEYS, 0:HEAD_DIM], query), axis=0, keepdims=True)
         query_out[u, HEAD_DIM:, :] = offset_rows(top)
 
     def one_view(u, block):
@@ -240,10 +241,11 @@
     def send(u):
         return pltpu.make_async_copy(sums.at[u], sums_out.at[u], sems.at[u])
 
-    @pl.loop(0, views)
-    def _(u):
-        one_view(u, span)
-        send(u).start()
+    @pl.loop(0, views // 2)
+    def _(i):
+        for u in (2 * i, 2 * i + 1):
+            one_view(u, span)
+            send(u).start()
 
     largest = jnp.max(sums[:, SUM_ROW : SUM_ROW + 1, :])
     for u in range(views):
@@ -413,8 +415,9 @@
         rows = packed[:, i * HEAD_DIM : (i + 1) * HEAD_DIM, :].reshape(HEADS * HEAD_DIM, tok)
         context[i * tok : (i + 1) * tok, :] = rows.T
     copies = []
-    cols = weight.shape[1] // 2
-    for j in range(2):
+    parts = sems.shape[0]
+    cols = weight.shape[1] // parts
+    for j in range(parts):
         at = slice(j * cols, (j + 1) * cols)
         blocks[:, :, at] = dot(context[...], weight[:, at]).astype(BF16).reshape(views, tok, cols)
         copies.append(pltpu.make_async_copy(blocks.at[:, :, at], out.at[:, :, at], sems.at[j]))
@@ -436,7 +439,7 @@
         scratch_shapes=[
             pltpu.VMEM((views * tok, width), BF16),
             pltpu.VMEM((views, tok, width), BF16),
-            pltpu.SemaphoreType.DMA((2,)),
+            pltpu.SemaphoreType.DMA((4,)),
         ],
         compiler_params=params(24),
         cost_estimate=cost(2 * views * tok * width * width, 4 * MIB),

time: 180 us -> 180 us (level)
  no operation moved by 1% of the time
where the time goes in v7:
time: 180 us; the launch traced here: 179 us
  Pallas kernels  140 us (78%)
  blocking collectives  15.8 us (9%)
  starting transfers between devices  11.3 us (6%)
  waiting for transfers between devices  10.4 us (6%)
  other arithmetic  2.09 us (1%)
    pallas_call x1, Pallas kernels, observed_part(): pl.pallas_call(observed_kernel, in_specs=[vmem], out_specs=[vmem, pl.Bloc...  72.7 us
    pallas_call x1, Pallas kernels, generated_part(): pl.pallas_call(generated_kernel, in_specs=[pl.BlockSpec(memory_space=pltp...  57.2 us
    all_to_all x1, blocking collectives, exchange(): lax.all_to_all(blocks, ('view', 'patch'), split_axis=0, concat_axis=0, ti...  15.8 us
    all_to_all x1, waiting for transfers between devices, exchange(): lax.all_to_all(blocks, ('view', 'patch'), split_axis=0, concat_axis=0, ti...  8.67 us
    all_to_all x1, starting transfers between devices, exchange(): lax.all_to_all(blocks, ('view', 'patch'), split_axis=0, concat_axis=0, ti...  7.11 us
    pallas_call x1, Pallas kernels, pack_pairs(): pl.pallas_call(pack_pairs_kernel, in_specs=[pl.BlockSpec(memory_space=plt...  4.63 us
    all_to_all x1, starting transfers between devices, on_device(): lax.all_to_all(pairs, 'patch', split_axis=0, concat_axis=0, tiled=True)  3.74 us
  transfers between devices with their start and end apart: 3, of which 2 were waited for; matrix products, arithmetic and copies ran while one was open for 1% of the time, Pallas kernels for 43%

profile of v7, /device:TPU:27, one launch (start us, length us, event | category | flops | bytes accessed | tf_op | source)
XLA Modules:
  0.0 179.4 jit_solution(7204044079699471040)
XLA Ops:
  0.0 3.6 %pack_queries.1 = bf16[16,320,128]{2,1,0:T(8,128)(2,1)} custom-call(s32[1]{0:T(128)} %bitcast.view, bf16[2,128,1024]{2,1,0:T(8,128)(2,1)} %hidden.3, bf16[2,128,1024]{2,1,0:T(8,128)(2,1)} %rays.3, bf16[1024,1024]{1,0:T(8,128)(2,1)} %weight.2, bf16[3,128,1024]{2,1,0:T(8,128)(2,1)} %obs_k.1, bf16[3,128,1024]{2,1,0:T(8,128)(2,1)} %obs_v.1), custom_call_target="tpu_custom_call" | custom-call | flops 536870912 | bytes 6291456 | tf_op jit(solution)/shard_map/pack_queries/pallas_call | solution.py:101
  3.6 7.1 %all-to-all-start = ((bf16[16,320,128]{2,1,0:T(8,128)(2,1)}), bf16[16,320,128]{2,1,0:T(8,128)(2,1)S(1)}, u32[]{:S(2)}, u32[]{:S(2)}) async-start(bf16[16,320,128]{2,1,0:T(8,128)(2,1)} %pack_queries.1), calls=%async_computation | async-start | bytes 2621440 | tf_op jit(solution)/shard_map/all_to_all | solution.py:451
  10.7 4.6 %pack_pairs.1 = (bf16[8,256,128]{2,1,0:T(8,128)(2,1)}, bf16[8,256,128]{2,1,0:T(8,128)(2,1)}) custom-call(s32[1]{0:T(128)} %bitcast.view, bf16[2,128,1024]{2,1,0:T(8,128)(2,1)} %hidden.3, bf16[2,128,1024]{2,1,0:T(8,128)(2,1)} %rays.3, bf16[1024,1024]{1,0:T(8,128)(2,1)} %w_key.1, bf16[1024,1024]{1,0:T(8,128)(2,1)} %w_value.1), custom_call_target="tpu_custom_call" | custom-call | flops 1073741824 | bytes 7340032 | tf_op jit(solution)/shard_map/pack_pairs/pallas_call | solution.py:154
  15.3 0.4 collective-permute-start
  15.8 1.8 collective-permute-done
  17.5 2.1 %pad_maximum_fusion = bf16[8,512,128]{2,1,0:T(8,128)(2,1)} fusion(bf16[8,256,128]{2,1,0:T(8,128)(2,1)S(1)} %collective-permute-done, bf16[8,256,128]{2,1,0:T(8,128)(2,1)} %get-tuple-element.11), kind=kLoop, calls=%fused_computation | loop fusion | flops 2097152 | bytes 2097152 | tf_op jit(solution)/shard_map/concatenate | solution.py:460
  19.6 8.7 %all-to-all-done.packed = bf16[16,320,128]{2,1,0:T(8,128)(2,1)S(1)} async-done(((bf16[16,320,128]{2,1,0:T(8,128)(2,1)}), bf16[16,320,128]{2,1,0:T(8,128)(2,1)S(1)}, u32[]{:S(2)}, u32[]{:S(2)}) %all-to-all-start) | async-done | bytes 1310752 | tf_op jit(solution)/shard_map/all_to_all | solution.py:451
  28.3 3.7 %all-to-all-start.1 = ((bf16[8,512,128]{2,1,0:T(8,128)(2,1)}), bf16[8,512,128]{2,1,0:T(8,128)(2,1)S(1)}, u32[]{:S(2)}, u32[]{:S(2)}) async-start(bf16[8,512,128]{2,1,0:T(8,128)(2,1)} %pad_maximum_fusion), calls=%async_computation.1 | async-start | bytes 2097152 | tf_op jit(solution)/shard_map/all_to_all | solution.py:461
  32.0 0.0 copy-start.1
  32.0 72.7 %observed_part.1 = (bf16[4,128,1024]{2,1,0:T(8,128)(2,1)S(1)}, f32[4,80,1024]{2,1,0:T(8,128)}) custom-call(bf16[16,320,128]{2,1,0:T(8,128)(2,1)S(1)} %all-to-all-done.packed), custom_call_target="tpu_custom_call" | custom-call | flops 6442450944 | bytes 4194304 | tf_op jit(solution)/shard_map/observed_part/pallas_call | solution.py:276
  104.7 0.0 all-to-all-done.1.packed
  104.7 0.0 copy-done.1
  104.7 0.0 copy-start
  104.8 57.2 %generated_part.1 = bf16[16,128,128]{2,1,0:T(8,128)(2,1)S(1)} custom-call(s32[4]{0:T(128)S(1)} %copy-done.1, s32[1]{0:T(128)} %bitcast.view, bf16[4,128,1024]{2,1,0:T(8,128)(2,1)S(1)} %get-tuple-element.9.query, f32[4,80,1024]{2,1,0:T(8,128)} %get-tuple-element.10.before, bf16[8,512,128]{2,1,0:T(8,128)(2,1)S(1)} %all-to-all-done.1.packed), custom_call_target="tpu_custom_call" | custom-call | flops 6442450944 | bytes 4194304 | tf_op jit(solution)/shard_map/generated_part/pallas_call | solution.py:387
  162.0 15.8 %all_to_all.15.packed = bf16[16,128,128]{2,1,0:T(8,128)(2,1)S(1)} all-to-all(bf16[16,128,128]{2,1,0:T(8,128)(2,1)S(1)} %generated_part.1), channel_id=1, replica_groups=mesh['group'=8,'view'=2,'patch'=8] {'view','patch'}, dimensions={0} | all-to-all | bytes 1048576 | tf_op jit(solution)/shard_map/all_to_all | solution.py:451
  177.8 0.0 copy-done
  177.8 1.5 project_out.1
Async XLA Ops:
  3.6 24.7 %all-to-all-start = ((bf16[16,320,128]{2,1,0:T(8,128)(2,1)}), bf16[16,320,128]{2,1,0:T(8,128)(2,1)S(1)}, u32[]{:S(2)}, u32[]{:S(2)}) async-start(bf16[16,320,128]{2,1,0:T(8,128)(2,1)} %pack_queries.1), calls=%async_computation | async-start | bytes 2621440 | tf_op jit(solution)/shard_map/all_to_all | solution.py:451
  15.3 2.2 %collective-permute-start = (bf16[8,256,128]{2,1,0:T(8,128)(2,1)}, bf16[8,256,128]{2,1,0:T(8,128)(2,1)S(1)}, u32[]{:S(2)}, u32[]{:S(2)}) collective-permute-start(bf16[8,256,128]{2,1,0:T(8,128)(2,1)} %get-tuple-element.12), channel_id=1, source_target_pairs={{0,8},{8,0},{1,9},{9,1},{2,10},{10,2},{3,11},{11,3},{4,12},{12,4},... | collective-permute-start | bytes 1572872 | tf_op jit(solution)/shard_map/ppermute | solution.py:459
  28.3 76.4 %all-to-all-start.1 = ((bf16[8,512,128]{2,1,0:T(8,128)(2,1)}), bf16[8,512,128]{2,1,0:T(8,128)(2,1)S(1)}, u32[]{:S(2)}, u32[]{:S(2)}) async-start(bf16[8,512,128]{2,1,0:T(8,128)(2,1)} %pad_maximum_fusion), calls=%async_computation.1 | async-start | bytes 2097152 | tf_op jit(solution)/shard_map/all_to_all | solution.py:461
  32.0 72.7 %copy-start.1 = (s32[4]{0:T(128)S(1)}, s32[4]{0:T(128)}, u32[]{:S(2)}) copy-start(s32[4]{0:T(128)} %view_set.1) | copy-start | bytes 52
  104.7 73.0 %copy-start = (bf16[1024,1024]{1,0:T(8,128)(2,1)S(1)}, bf16[1024,1024]{1,0:T(8,128)(2,1)}, u32[]{:S(2)}) copy-start(bf16[1024,1024]{1,0:T(8,128)(2,1)} %weight.3) | copy-start | bytes 6291460

commit v8 on v4

--- a/solution.py
+++ b/solution.py
@@ -10,6 +10,7 @@
 SUM_ROW = HEAD_DIM
 VALUE_ROWS = HEAD_DIM + 16
 KEY_COLS = 2 * HEAD_DIM
+FIRST_KEYS = 32
 LIMIT = 2.0**100
 BF16 = jnp.bfloat16
 F32 = jnp.float32
@@ -226,7 +227,7 @@
         rows = slice((u % here) * HEAD_DIM, (u % here + 1) * HEAD_DIM)
         query = jnp.concatenate([packed[(u // here) * patches + p, rows, :] for p in range(patches)], axis=1)
         query_out[u, 0:HEAD_DIM, :] = query
-        top = jnp.max(dot(keys[0:tok, 0:HEAD_DIM], query), axis=0, keepdims=True)
+        top = jnp.max(dot(keys[0:FIRST_KEYS, 0:HEAD_DIM], query), axis=0, keepdims=True)
         query_out[u, HEAD_DIM:, :] = offset_rows(top)
 
     def one_view(u, block):
@@ -363,7 +364,7 @@
 
     for u in range(views):
         total = sums[u] + early[u]
-        context = (total[0:HEAD_DIM] / total[SUM_ROW : SUM_ROW + 1]).astype(BF16)
+        context = (total[0:HEAD_DIM] * (1.0 / total[SUM_ROW : SUM_ROW + 1])).astype(BF16)
         rows = slice((u % here) * HEAD_DIM, (u % here + 1) * HEAD_DIM)
         for p in range(patches):
             out[(u // here) * patches + p, rows, :] = context[:, p * tok : (p + 1) * tok]

time: 180 us -> 180 us (level)
  Pallas kernels: 79.6 us -> 140 us
  blocking collectives: 75 us -> 15.8 us
    pallas_call x1, Pallas kernels: 12.7 us -> 73 us  [observed_part(): pl.pallas_call(observed_kernel, in_specs=[vmem], out_specs=[vmem, pl.Bloc...]
    all_to_all x1, blocking collectives: 75 us -> 15.8 us  [exchange(): lax.all_to_all(blocks, ('view', 'patch'), split_axis=0, concat_axis=0, ti...]
  transfers between devices with their start and end apart: 3 -> 3, of which waited for: 3 -> 2; matrix products, arithmetic and copies ran while one was open for 1% -> 1% of each run, Pallas kernels for 10% -> 43%
where the time goes in v8:
time: 180 us
  Pallas kernels  140 us (78%)
  blocking collectives  15.8 us (9%)
  starting transfers between devices  11.3 us (6%)
  waiting for transfers between devices  10.4 us (6%)
  other arithmetic  2.09 us (1%)
    pallas_call x1, Pallas kernels, observed_part(): pl.pallas_call(observed_kernel, in_specs=[vmem], out_specs=[vmem, pl.Bloc...  73 us
    pallas_call x1, Pallas kernels, generated_part(): pl.pallas_call(generated_kernel, in_specs=[pl.BlockSpec(memory_space=pltp...  57.3 us
    all_to_all x1, blocking collectives, exchange(): lax.all_to_all(blocks, ('view', 'patch'), split_axis=0, concat_axis=0, ti...  15.8 us
    all_to_all x1, waiting for transfers between devices, exchange(): lax.all_to_all(blocks, ('view', 'patch'), split_axis=0, concat_axis=0, ti...  8.67 us
    all_to_all x1, starting transfers between devices, exchange(): lax.all_to_all(blocks, ('view', 'patch'), split_axis=0, concat_axis=0, ti...  7.11 us
    pallas_call x1, Pallas kernels, pack_pairs(): pl.pallas_call(pack_pairs_kernel, in_specs=[pl.BlockSpec(memory_space=plt...  4.63 us
    all_to_all x1, starting transfers between devices, on_device(): lax.all_to_all(pairs, 'patch', split_axis=0, concat_axis=0, tiled=True)  3.74 us
  transfers between devices with their start and end apart: 3, of which 2 were waited for; matrix products, arithmetic and copies ran while one was open for 1% of the time, Pallas kernels for 43%

profile of v8, /device:TPU:27, one launch (start us, length us, event | category | flops | bytes accessed | tf_op | source)
XLA Modules:
  0.0 179.6 jit_solution(6106178173422658890)
XLA Ops:
  0.0 3.6 %pack_queries.1 = bf16[16,320,128]{2,1,0:T(8,128)(2,1)} custom-call(s32[1]{0:T(128)} %bitcast.view, bf16[2,128,1024]{2,1,0:T(8,128)(2,1)} %hidden.3, bf16[2,128,1024]{2,1,0:T(8,128)(2,1)} %rays.3, bf16[1024,1024]{1,0:T(8,128)(2,1)} %weight.2, bf16[3,128,1024]{2,1,0:T(8,128)(2,1)} %obs_k.1, bf16[3,128,1024]{2,1,0:T(8,128)(2,1)} %obs_v.1), custom_call_target="tpu_custom_call" | custom-call | flops 536870912 | bytes 6291456 | tf_op jit(solution)/shard_map/pack_queries/pallas_call | solution.py:101
  3.6 7.1 %all-to-all-start = ((bf16[16,320,128]{2,1,0:T(8,128)(2,1)}), bf16[16,320,128]{2,1,0:T(8,128)(2,1)S(1)}, u32[]{:S(2)}, u32[]{:S(2)}) async-start(bf16[16,320,128]{2,1,0:T(8,128)(2,1)} %pack_queries.1), calls=%async_computation | async-start | bytes 2621440 | tf_op jit(solution)/shard_map/all_to_all | solution.py:440
  10.7 4.6 %pack_pairs.1 = (bf16[8,256,128]{2,1,0:T(8,128)(2,1)}, bf16[8,256,128]{2,1,0:T(8,128)(2,1)}) custom-call(s32[1]{0:T(128)} %bitcast.view, bf16[2,128,1024]{2,1,0:T(8,128)(2,1)} %hidden.3, bf16[2,128,1024]{2,1,0:T(8,128)(2,1)} %rays.3, bf16[1024,1024]{1,0:T(8,128)(2,1)} %w_key.1, bf16[1024,1024]{1,0:T(8,128)(2,1)} %w_value.1), custom_call_target="tpu_custom_call" | custom-call | flops 1073741824 | bytes 7340032 | tf_op jit(solution)/shard_map/pack_pairs/pallas_call | solution.py:154
  15.3 0.4 collective-permute-start
  15.8 1.8 collective-permute-done
  17.5 2.1 %pad_maximum_fusion = bf16[8,512,128]{2,1,0:T(8,128)(2,1)} fusion(bf16[8,256,128]{2,1,0:T(8,128)(2,1)S(1)} %collective-permute-done, bf16[8,256,128]{2,1,0:T(8,128)(2,1)} %get-tuple-element.11), kind=kLoop, calls=%fused_computation | loop fusion | flops 2097152 | bytes 2097152 | tf_op jit(solution)/shard_map/concatenate | solution.py:449
  19.6 8.7 %all-to-all-done.packed = bf16[16,320,128]{2,1,0:T(8,128)(2,1)S(1)} async-done(((bf16[16,320,128]{2,1,0:T(8,128)(2,1)}), bf16[16,320,128]{2,1,0:T(8,128)(2,1)S(1)}, u32[]{:S(2)}, u32[]{:S(2)}) %all-to-all-start) | async-done | bytes 1310752 | tf_op jit(solution)/shard_map/all_to_all | solution.py:440
  28.3 3.7 %all-to-all-start.1 = ((bf16[8,512,128]{2,1,0:T(8,128)(2,1)}), bf16[8,512,128]{2,1,0:T(8,128)(2,1)S(1)}, u32[]{:S(2)}, u32[]{:S(2)}) async-start(bf16[8,512,128]{2,1,0:T(8,128)(2,1)} %pad_maximum_fusion), calls=%async_computation.1 | async-start | bytes 2097152 | tf_op jit(solution)/shard_map/all_to_all | solution.py:450
  32.0 0.0 copy-start.1
  32.0 73.0 %observed_part.1 = (bf16[4,128,1024]{2,1,0:T(8,128)(2,1)S(1)}, f32[4,80,1024]{2,1,0:T(8,128)}) custom-call(bf16[16,320,128]{2,1,0:T(8,128)(2,1)S(1)} %all-to-all-done.packed), custom_call_target="tpu_custom_call" | custom-call | flops 6442450944 | bytes 4194304 | tf_op jit(solution)/shard_map/observed_part/pallas_call | solution.py:275
  105.0 0.0 all-to-all-done.1.packed
  105.0 0.0 copy-done.1
  105.0 0.0 copy-start
  105.1 57.3 %generated_part.1 = bf16[16,128,128]{2,1,0:T(8,128)(2,1)S(1)} custom-call(s32[4]{0:T(128)S(1)} %copy-done.1, s32[1]{0:T(128)} %bitcast.view, bf16[4,128,1024]{2,1,0:T(8,128)(2,1)S(1)} %get-tuple-element.9.query, f32[4,80,1024]{2,1,0:T(8,128)} %get-tuple-element.10.before, bf16[8,512,128]{2,1,0:T(8,128)(2,1)S(1)} %all-to-all-done.1.packed), custom_call_target="tpu_custom_call" | custom-call | flops 6442450944 | bytes 4194304 | tf_op jit(solution)/shard_map/generated_part/pallas_call | solution.py:377
  162.3 15.8 %all_to_all.15.packed = bf16[16,128,128]{2,1,0:T(8,128)(2,1)S(1)} all-to-all(bf16[16,128,128]{2,1,0:T(8,128)(2,1)S(1)} %generated_part.1), channel_id=1, replica_groups=mesh['group'=8,'view'=2,'patch'=8] {'view','patch'}, dimensions={0} | all-to-all | bytes 1048576 | tf_op jit(solution)/shard_map/all_to_all | solution.py:440
  178.1 0.0 copy-done
  178.1 1.5 project_out.1
Async XLA Ops:
  3.6 24.7 %all-to-all-start = ((bf16[16,320,128]{2,1,0:T(8,128)(2,1)}), bf16[16,320,128]{2,1,0:T(8,128)(2,1)S(1)}, u32[]{:S(2)}, u32[]{:S(2)}) async-start(bf16[16,320,128]{2,1,0:T(8,128)(2,1)} %pack_queries.1), calls=%async_computation | async-start | bytes 2621440 | tf_op jit(solution)/shard_map/all_to_all | solution.py:440
  15.3 2.2 %collective-permute-start = (bf16[8,256,128]{2,1,0:T(8,128)(2,1)}, bf16[8,256,128]{2,1,0:T(8,128)(2,1)S(1)}, u32[]{:S(2)}, u32[]{:S(2)}) collective-permute-start(bf16[8,256,128]{2,1,0:T(8,128)(2,1)} %get-tuple-element.12), channel_id=1, source_target_pairs={{0,8},{8,0},{1,9},{9,1},{2,10},{10,2},{3,11},{11,3},{4,12},{12,4},... | collective-permute-start | bytes 1572872 | tf_op jit(solution)/shard_map/ppermute | solution.py:448
  28.3 76.7 %all-to-all-start.1 = ((bf16[8,512,128]{2,1,0:T(8,128)(2,1)}), bf16[8,512,128]{2,1,0:T(8,128)(2,1)S(1)}, u32[]{:S(2)}, u32[]{:S(2)}) async-start(bf16[8,512,128]{2,1,0:T(8,128)(2,1)} %pad_maximum_fusion), calls=%async_computation.1 | async-start | bytes 2097152 | tf_op jit(solution)/shard_map/all_to_all | solution.py:450
  32.0 73.0 %copy-start.1 = (s32[4]{0:T(128)S(1)}, s32[4]{0:T(128)}, u32[]{:S(2)}) copy-start(s32[4]{0:T(128)} %view_set.1) | copy-start | bytes 52
  105.0 73.1 %copy-start = (bf16[1024,1024]{1,0:T(8,128)(2,1)S(1)}, bf16[1024,1024]{1,0:T(8,128)(2,1)}, u32[]{:S(2)}) copy-start(bf16[1024,1024]{1,0:T(8,128)(2,1)} %weight.3) | copy-start | bytes 6291460
